TPU v7x, 128 devices: a whole 4x4x4 slice. The times are simulated.
128 devices in a mesh: src: 8 (over y, core), tgt: 16 (over z, x).
Axes of the slice: x: 4, y: 4, z: 4, core: 2. Of those that a mesh axis runs over, the one named last changes fastest.
Arguments:
- node_feats: bfloat16 [131072, 256], P(('src', 'tgt')), may hold values from -6 to 6
- send_block: int32 [128, 128, 2], P(('src', 'tgt')), may hold values from 0 to 7
- recv_block: int32 [128, 128, 2], P(('src', 'tgt')), may hold values from 0 to 7
- recv_rel: int32 [128, 128, 2], P(('src', 'tgt')), may hold values from 0 to 29
- recv_count: int32 [128, 128], P(('src', 'tgt')), may hold values from 0 to 2, as said below
- recv_adj: bfloat16 [128, 128, 2, 128, 128], P(('src', 'tgt')), may hold values from 0.1 to 100, as said below
- local_src: int32 [128, 64], P(('src', 'tgt')), may hold values from 0 to 7
- local_tgt: int32 [128, 64], P(('src', 'tgt')), may hold values from 0 to 7
- local_rel: int32 [128, 64], P(('src', 'tgt')), may hold values from 0 to 29
- local_adj: bfloat16 [128, 64, 128, 128], P(('src', 'tgt')), may hold values from 0.1 to 100, as said below
- bases: bfloat16 [8, 256, 256], replicated, may hold values from -0.375 to 0.375
- coeffs: bfloat16 [30, 8], replicated, may hold values from -2 to 2
- self_weight: bfloat16 [256, 256], replicated, may hold values from -0.375 to 0.375
- cotangent: bfloat16 [131072, 256], P(('src', 'tgt')), may hold values from -6 to 6
Outputs:
- features_out: bfloat16 [131072, 256], P(('src', 'tgt'))
- grad_features: bfloat16 [131072, 256], P(('src', 'tgt'))
- grad_bases: float32 [8, 256, 256], replicated
- grad_coef: float32 [30, 8], replicated
- grad_self: float32 [256, 256], replicated
Inputs may be any that keep to these rules, and one draw needn't show every extreme that they name: Only the first recv_count[q, p] slots from band p to band q are valid; in every draw some band takes 2 valid slots from every band. `recv_adj`: positive edge weights. `local_adj`: positive edge weights.
All inputs are finite; a program needn't handle non-finite values.
Results may differ from a plain program's by a relative error of at most 0.0068.
Values may be sent and summed in bfloat16 or wider, within the bound.
A program may use at most 256 MiB of HBM per device.

v0:
```python
import math

import jax
import jax.numpy as jnp
from jax import lax
from jax.sharding import PartitionSpec as P


def slot_tables(target_ids, relation_ids, valid_mask, coeffs, block_count):
    onehot_tgt = (target_ids[:, None] == jnp.arange(block_count, dtype=jnp.int32)[None, :]).astype(
        jnp.float32
    ) * valid_mask[:, None]
    relations = coeffs.shape[0]
    onehot_rel = (relation_ids[:, None] == jnp.arange(relations, dtype=jnp.int32)[None, :]).astype(
        jnp.bfloat16
    )
    coef_rows = jnp.dot(onehot_rel, coeffs, preferred_element_type=jnp.float32)
    mixing = (
        (onehot_tgt[:, :, None] * coef_rows[:, None, :])
        .reshape(target_ids.shape[0], -1)
        .astype(jnp.bfloat16)
    )
    return (onehot_tgt, onehot_rel.astype(jnp.float32), mixing)


def aggregate(adjacency, src_rows, valid_mask, tables):
    onehot_tgt, onehot_rel, mixing = tables
    aggregated = (
        jnp.einsum("sij,sjh->sih", adjacency, src_rows, preferred_element_type=jnp.float32)
        * valid_mask[:, None, None]
    ).astype(jnp.bfloat16)
    agg_flat = aggregated.reshape(aggregated.shape[0], -1)
    basis_part = lax.dot_general(
        mixing, agg_flat, (((0,), (0,)), ((), ())), preferred_element_type=jnp.float32
    )
    weight_rows = jnp.sum(adjacency, axis=2, dtype=jnp.float32)
    degree = lax.dot_general(
        onehot_tgt,
        weight_rows,
        (((0,), (0,)), ((), ())),
        precision=lax.Precision.HIGHEST,
        preferred_element_type=jnp.float32,
    )
    return (agg_flat, basis_part, degree)


def backward_slots(adjacency, agg_flat, valid_mask, tables, proj_flat, block_count):
    onehot_tgt, onehot_rel, mixing = tables
    pair_prods = lax.dot_general(
        agg_flat, proj_flat, (((1,), (1,)), ((), ())), preferred_element_type=jnp.float32
    )
    inner_prod = jnp.sum(
        pair_prods.reshape(agg_flat.shape[0], block_count, -1) * onehot_tgt[:, :, None], axis=1
    )
    coef_grad = lax.dot_general(
        onehot_rel,
        inner_prod,
        (((0,), (0,)), ((), ())),
        precision=lax.Precision.HIGHEST,
        preferred_element_type=jnp.float32,
    )
    slot_cot = jnp.dot(mixing, proj_flat, preferred_element_type=jnp.float32).astype(jnp.bfloat16)
    slot_cot = slot_cot.reshape(adjacency.shape[0], adjacency.shape[1], -1)
    slot_grad = (
        jnp.einsum("sij,sih->sjh", adjacency, slot_cot, preferred_element_type=jnp.float32)
        * valid_mask[:, None, None]
    ).astype(jnp.bfloat16)
    return (coef_grad, slot_grad)


def local(
    node_feats,
    send_block,
    recv_block,
    recv_rel,
    recv_count,
    recv_adj,
    local_src,
    local_tgt,
    local_rel,
    local_adj,
    bases,
    coeffs,
    self_weight,
    cotangent,
):
    peer_count = lax.axis_size(("src", "tgt"))
    node_rows, feat_width = node_feats.shape
    block_rows = recv_adj.shape[-1]
    block_count = node_rows // block_rows
    slot_cap = send_block.shape[2]
    remote = peer_count * slot_cap
    basis_count = bases.shape[0]
    node_blocks = node_feats.reshape(block_count, block_rows, feat_width)
    outgoing = node_blocks[send_block[0]]
    incoming = lax.all_to_all(outgoing, ("src", "tgt"), split_axis=0, concat_axis=0, tiled=True)
    incoming = incoming.reshape(remote, block_rows, feat_width)
    local_count = local_src.shape[1]
    local_valid = jnp.ones((local_count,), jnp.float32)
    local_tables = slot_tables(local_tgt[0], local_rel[0], local_valid, coeffs, block_count)
    local_flat, local_part, local_degree = aggregate(
        local_adj[0], node_blocks[local_src[0]], local_valid, local_tables
    )
    remote_valid = (
        (jnp.arange(slot_cap, dtype=jnp.int32)[None, :] < recv_count[0][:, None])
        .astype(jnp.float32)
        .reshape(remote)
    )
    remote_adj = recv_adj[0].reshape(remote, block_rows, block_rows)
    remote_tables = slot_tables(
        recv_block[0].reshape(remote),
        recv_rel[0].reshape(remote),
        remote_valid,
        coeffs,
        block_count,
    )
    remote_flat, remote_part, remote_degree = aggregate(
        remote_adj, incoming, remote_valid, remote_tables
    )
    row_norm = lax.rsqrt(1.0 + local_degree + remote_degree)
    basis_sums = (
        (local_part + remote_part)
        .astype(jnp.bfloat16)
        .reshape(block_count, basis_count, block_rows, feat_width)
    )
    mixed_sum = jnp.einsum("tbih,bhk->tik", basis_sums, bases, preferred_element_type=jnp.float32)
    self_term = jnp.dot(node_feats, self_weight, preferred_element_type=jnp.float32).reshape(
        block_count, block_rows, feat_width
    )
    features_out = (
        (row_norm[:, :, None] * mixed_sum + self_term)
        .astype(jnp.bfloat16)
        .reshape(node_rows, feat_width)
    )
    scaled = (row_norm[:, :, None] * cotangent.reshape(block_count, block_rows, feat_width)).astype(
        jnp.bfloat16
    )
    projected = jnp.einsum(
        "tik,bhk->tbih", scaled, bases, preferred_element_type=jnp.float32
    ).astype(jnp.bfloat16)
    proj_flat = projected.reshape(block_count * basis_count, block_rows * feat_width)
    grad_bases = jnp.einsum("tbih,tik->bhk", basis_sums, scaled, preferred_element_type=jnp.float32)
    remote_coef, remote_grad = backward_slots(
        remote_adj, remote_flat, remote_valid, remote_tables, proj_flat, block_count
    )
    returned = lax.all_to_all(
        remote_grad.reshape(peer_count, slot_cap, block_rows, feat_width),
        ("src", "tgt"),
        split_axis=0,
        concat_axis=0,
        tiled=True,
    )
    returned = returned.reshape(remote, block_rows * feat_width)
    local_coef, local_grad = backward_slots(
        local_adj[0], local_flat, local_valid, local_tables, proj_flat, block_count
    )
    block_ids = jnp.arange(block_count, dtype=jnp.int32)[None, :]
    send_hot = (send_block[0].reshape(remote)[:, None] == block_ids).astype(jnp.bfloat16)
    local_hot = (local_src[0][:, None] == block_ids).astype(jnp.bfloat16)
    gathered = lax.dot_general(
        send_hot, returned, (((0,), (0,)), ((), ())), preferred_element_type=jnp.float32
    )
    gathered = gathered + lax.dot_general(
        local_hot,
        local_grad.reshape(local_count, -1),
        (((0,), (0,)), ((), ())),
        preferred_element_type=jnp.float32,
    )
    self_back = lax.dot_general(
        cotangent, self_weight, (((1,), (1,)), ((), ())), preferred_element_type=jnp.float32
    )
    grad_features = (gathered.reshape(node_rows, feat_width) + self_back).astype(jnp.bfloat16)
    grad_self = lax.dot_general(
        node_feats, cotangent, (((0,), (0,)), ((), ())), preferred_element_type=jnp.float32
    )
    totals = lax.psum((grad_bases, local_coef + remote_coef, grad_self), ("src", "tgt"))
    grad_scale = 1.0 / math.sqrt(node_rows * peer_count)
    return (
        features_out,
        grad_features,
        totals[0] * grad_scale,
        totals[1] * grad_scale,
        totals[2] * grad_scale,
    )


def solution(mesh):
    in_specs = (
        P(("src", "tgt"), None),
        P(("src", "tgt"), None, None),
        P(("src", "tgt"), None, None),
        P(("src", "tgt"), None, None),
        P(("src", "tgt"), None),
        P(("src", "tgt"), None, None, None, None),
        P(("src", "tgt"), None),
        P(("src", "tgt"), None),
        P(("src", "tgt"), None),
        P(("src", "tgt"), None, None, None),
        P(),
        P(),
        P(),
        P(("src", "tgt"), None),
    )
    out_specs = (P(("src", "tgt"), None), P(("src", "tgt"), None), P(), P(), P())
    return jax.shard_map(local, mesh=mesh, in_specs=in_specs, out_specs=out_specs, check_vma=False)
```

profile of v0, /device:TPU:1, one launch (start us, length us, event | category | flops | bytes accessed | tf_op | source)
XLA Modules:
  0.0 767.2 jit_solution(7694763770230259879)
XLA Ops:
  8.2 10.7 %gather_fusion.1 = bf16[256,128,256]{2,1,0:T(8,128)(2,1)} fusion(bf16[8,128,256]{2,1,0:T(8,128)(2,1)} %bitcast.146, s32[1024]{0:T(1024)S(1)} %pad_clamp_fusion), kind=kCustom, calls=%fused_computation.1 | custom fusion | bytes 33555456 | tf_op jit(solution)/shard_map/gather | solution.py:95
  19.0 22.4 %copy.45 = bf16[128,2,128,256]{2,3,1,0:T(8,128)(2,1)} copy(bf16[128,2,128,256]{3,2,1,0:T(8,128)(2,1)} %bitcast.154) | data formatting | bytes 33554432 | tf_op jit(solution)/shard_map/gather | solution.py:95
  41.4 12.7 %all-to-all-start = ((bf16[128,2,128,256]{2,3,1,0:T(8,128)(2,1)}), bf16[128,2,128,256]{2,3,1,0:T(8,128)(2,1)}, u32[]{:S(2)}, u32[]{:S(2)}) async-start(bf16[128,2,128,256]{2,3,1,0:T(8,128)(2,1)} %copy.45), calls=%async_computation | async-start | bytes 33554432 | tf_op jit(solution)/shard_map/all_to_all | solution.py:96
  55.3 5.8 convert_reduce_fusion
  64.7 4.6 copy.67
  70.4 7.0 convolution_convert_fusion
  77.4 7.9 %copy.68 = bf16[32,8,128,256]{3,2,1,0:T(8,128)(2,1)} copy(bf16[32,8,128,256]{3,1,2,0:T(8,128)(2,1)S(1)} %bitcast.155) | data formatting | bytes 33554432
  85.3 18.5 %multiply_convert_fusion = bf16[256,256,128]{2,1,0:T(8,128)(2,1)} fusion(f32[256]{0:T(256)S(1)} %reshape.269, bf16[256,128,256]{2,1,0:T(8,128)(2,1)} %bitcast.151, bf16[256,128,128]{2,1,0:T(8,128)(2,1)} %bitcast.149), kind=kOutput, calls=%fused_computation.7 | convolution fusion | flops 2164260864 | bytes 41944064 | tf_op jit(solution)/shard_map/sij,sih->sjh/dot_general | solution.py:65
  103.9 22.3 %copy.50 = bf16[128,2,128,256]{3,2,1,0:T(8,128)(2,1)} copy(bf16[128,2,128,256]{2,3,1,0:T(8,128)(2,1)} %bitcast.152) | data formatting | bytes 33554432 | tf_op jit(solution)/shard_map/reshape | solution.py:147
  126.2 163.5 %all-to-all-done = bf16[128,2,128,256]{2,3,1,0:T(8,128)(2,1)} async-done(((bf16[128,2,128,256]{2,3,1,0:T(8,128)(2,1)}), bf16[128,2,128,256]{2,3,1,0:T(8,128)(2,1)}, u32[]{:S(2)}, u32[]{:S(2)}) %all-to-all-start) | async-done | bytes 16777248 | tf_op jit(solution)/shard_map/all_to_all | solution.py:96
  289.7 17.2 %all-to-all-start.1 = ((bf16[128,2,128,256]{3,2,1,0:T(8,128)(2,1)}), bf16[128,2,128,256]{3,2,1,0:T(8,128)(2,1)}, u32[]{:S(2)}, u32[]{:S(2)}) async-start(bf16[128,2,128,256]{3,2,1,0:T(8,128)(2,1)} %copy.50), calls=%async_computation.1 | async-start | bytes 33554432 | tf_op jit(solution)/shard_map/all_to_all | solution.py:146
  307.4 3.5 convolution_convert_fusion.1
  312.5 3.4 convert_bitcast_fusion
  315.9 7.1 copy.71
  323.0 2.8 gather_fusion
  325.7 6.2 convert_bitcast_fusion.2
  332.0 6.8 copy.54
  338.8 6.8 copy.66
  345.5 8.3 %fusion.43 = f32[64,8]{0,1:T(8,128)S(1)} fusion(bf16[64,128,256]{2,0,1:T(8,128)(2,1)} %copy.54, f32[64,8]{0,1:T(8,128)S(1)} %fusion.82, bf16[8,8,128,256]{3,2,1,0:T(8,128)(2,1)} %copy-done.4), kind=kOutput, calls=%fused_computation.37 | convolution fusion | flops 268443136 | bytes 8392704 | tf_op jit(solution)/shard_map/dot_general | solution.py:49
  356.4 4.5 fusion.72
  360.9 24.0 %fusion.1 = bf16[256,128,256]{1,2,0:T(8,128)(2,1)} fusion(f32[256]{0:T(256)S(1)} %reshape.269, bf16[256,128,256]{1,2,0:T(8,128)(2,1)} %bitcast.20, bf16[256,128,128]{2,1,0:T(8,128)(2,1)} %bitcast.150), kind=kOutput, calls=%fused_computation.9 | convolution fusion | flops 2164260864 | bytes 41944064 | tf_op jit(solution)/shard_map/sij,sjh->sih/dot_general | solution.py:29
  384.9 23.5 %copy.56 = bf16[256,128,256]{2,0,1:T(8,128)(2,1)} copy(bf16[256,128,256]{1,2,0:T(8,128)(2,1)} %fusion.1) | data formatting | bytes 33554432 | tf_op jit(solution)/shard_map/convert_element_type | solution.py:31
  408.4 24.2 %copy.46 = bf16[256,128,256]{0,2,1:T(8,128)(2,1)} copy(bf16[256,128,256]{1,2,0:T(8,128)(2,1)} %fusion.1) | data formatting | bytes 33554432 | tf_op jit(solution)/shard_map/convert_element_type | solution.py:31
  432.6 106.7 %all-to-all-done.1 = bf16[128,2,128,256]{3,2,1,0:T(8,128)(2,1)} async-done(((bf16[128,2,128,256]{3,2,1,0:T(8,128)(2,1)}), bf16[128,2,128,256]{3,2,1,0:T(8,128)(2,1)}, u32[]{:S(2)}, u32[]{:S(2)}) %all-to-all-start.1) | async-done | bytes 16777248 | tf_op jit(solution)/shard_map/all_to_all | solution.py:146
  539.3 16.3 %copy.69 = bf16[32,8,128,256]{3,1,2,0:T(8,128)(2,1)S(1)} copy(bf16[32,8,128,256]{3,2,1,0:T(8,128)(2,1)} %bitcast.53) | data formatting | bytes 33554432
  562.2 12.7 %fusion.34 = f32[256,8]{0,1:T(8,128)S(1)} fusion(bf16[256,128,256]{2,0,1:T(8,128)(2,1)} %copy.56, f32[256,8]{0,1:T(8,128)S(1)} %fusion.81, bf16[8,8,128,256]{3,2,1,0:T(8,128)(2,1)} %copy-done.4), kind=kOutput, calls=%fused_computation.34 | convolution fusion | flops 1073772544 | bytes 20987904 | tf_op jit(solution)/shard_map/dot_general | solution.py:49
  574.9 11.0 %fusion = bf16[64,32768]{1,0:T(8,128)(2,1)S(1)} fusion(f32[64,32768]{1,0:T(8,128)} %fusion.72, bf16[256,32768]{0,1:T(8,128)(2,1)} %bitcast.148, f32[256,8]{0,1:T(8,128)S(1)} %copy-done.12, f32[256,8]{0,1:T(8,128)S(1)} %fusion.81), kind=kOutput, calls=%fused_computation.4 | convolution fusion | flops 1077968896 | bytes 29376512 | tf_op jit(solution)/shard_map/dot_general | solution.py:33
  587.9 3.4 fusion.12
  591.5 78.1 %psum.22 = f32[30,8]{0,1:T(8,128)S(1)} all-reduce(f32[30,8]{0,1:T(8,128)S(1)} %convolution_add_fusion.4), channel_id=1, replica_groups=mesh['src'=8,'tgt'=16] {'src','tgt'}, use_global_device_ids=true, to_apply=%region_5.0 | all-reduce | flops 240 | bytes 1920 | tf_op jit(solution)/shard_map/psum | solution.py:176
  672.5 4.7 fusion.24
  677.2 79.1 %all-reduce.3.cloned.1.call-done = (f32[8,256,256]{2,1,0:T(8,128)}, f32[256,256]{1,0:T(8,128)}) async-done(((f32[8,256,256]{2,1,0:T(8,128)}, f32[256,256]{1,0:T(8,128)}), (f32[8,256,256]{2,1,0:T(8,128)}, f32[256,256]{1,0:T(8,128)})) %all-reduce.3.cloned.1.call-update) | async-done | bytes 2359312 | tf_op jit(solution)/shard_map/psum | solution.py:176
  756.3 3.1 broadcast_multiply_fusion
  (89 shorter events, 24.0 us)
Async XLA Ops:
  7.2 54.2 %copy-start = (bf16[8,256,256]{2,1,0:T(8,128)(2,1)S(1)}, bf16[8,256,256]{2,1,0:T(8,128)(2,1)}, u32[]{:S(2)}) copy-start(bf16[8,256,256]{2,1,0:T(8,128)(2,1)} %param.24) | copy-start | bytes 3145732
  41.4 12.7 %copy-start.22 = (s32[1,128]{1,0:T(1,128)S(1)}, s32[1,128]{1,0:T(1,128)}, u32[]{:S(2)}) copy-start(s32[1,128]{1,0:T(1,128)} %param.18) | copy-start | bytes 1540
  41.4 13.0 %copy-start.18 = (s32[1,128,2]{1,2,0:T(2,128)S(1)}, s32[1,128,2]{1,2,0:T(2,128)}, u32[]{:S(2)}) copy-start(s32[1,128,2]{1,2,0:T(2,128)} %param.16) | copy-start | bytes 3076
  41.4 13.2 %copy-start.2 = (bf16[1,64,128,128]{3,2,1,0:T(8,128)(2,1)S(1)}, bf16[1,64,128,128]{3,2,1,0:T(8,128)(2,1)}, u32[]{:S(2)}) copy-start(bf16[1,64,128,128]{3,2,1,0:T(8,128)(2,1)} %param.23) | copy-start | bytes 6291460
  41.4 248.3 %all-to-all-start = ((bf16[128,2,128,256]{2,3,1,0:T(8,128)(2,1)}), bf16[128,2,128,256]{2,3,1,0:T(8,128)(2,1)}, u32[]{:S(2)}, u32[]{:S(2)}) async-start(bf16[128,2,128,256]{2,3,1,0:T(8,128)(2,1)} %copy.45), calls=%async_computation | async-start | bytes 33554432 | tf_op jit(solution)/shard_map/all_to_all | solution.py:96
  55.3 6.0 copy-start.16
  55.3 6.1 copy-start.8
  61.4 1.3 copy-start.13
  62.7 2.0 copy-start.4
  64.7 4.6 copy-start.19
  64.7 4.9 copy-start.24
  69.6 0.9 copy-start.20
  126.2 180.7 %copy-start.15 = (s32[1,128,2]{1,2,0:T(2,128)S(1)}, s32[1,128,2]{1,2,0:T(2,128)}, u32[]{:S(2)}) copy-start(s32[1,128,2]{1,2,0:T(2,128)} %param.15) | copy-start | bytes 3076
  126.2 181.0 %copy-start.17 = (s32[1,64]{1,0:T(1,128)S(1)}, s32[1,64]{1,0:T(1,128)}, u32[]{:S(2)}) copy-start(s32[1,64]{1,0:T(1,128)} %param.21) | copy-start | bytes 772
  126.2 181.0 %copy-start.25 = (bf16[30,8]{0,1:T(8,128)(2,1)S(1)}, bf16[30,8]{0,1:T(8,128)(2,1)}, u32[]{:S(2)}) copy-start(bf16[30,8]{0,1:T(8,128)(2,1)} %param.25) | copy-start | bytes 1444
  126.2 181.0 %copy-start.26 = (s32[1,64]{1,0:T(1,128)S(1)}, s32[1,64]{1,0:T(1,128)}, u32[]{:S(2)}) copy-start(s32[1,64]{1,0:T(1,128)} %param.22) | copy-start | bytes 772
  289.7 249.6 %all-to-all-start.1 = ((bf16[128,2,128,256]{3,2,1,0:T(8,128)(2,1)}), bf16[128,2,128,256]{3,2,1,0:T(8,128)(2,1)}, u32[]{:S(2)}, u32[]{:S(2)}) async-start(bf16[128,2,128,256]{3,2,1,0:T(8,128)(2,1)} %copy.50), calls=%async_computation.1 | async-start | bytes 33554432 | tf_op jit(solution)/shard_map/all_to_all | solution.py:146
  306.9 449.4 %all-reduce.3.cloned.1.call-start = ((), (), s32[]{:S(2)}) async-start(), calls=%async_computation.2 | async-start | bytes 4718592 | tf_op jit(solution)/shard_map/psum | solution.py:176
  310.9 1.6 copy-start.3
  315.9 7.1 copy-start.23
  315.9 7.1 copy-start.1
  345.5 8.5 %copy-start.9 = (bf16[1024,256]{1,0:T(8,128)(2,1)S(1)}, bf16[1024,256]{1,0:T(8,128)(2,1)}, u32[]{:S(2)}) copy-start(bf16[1024,256]{1,0:T(8,128)(2,1)} %param.27) | copy-start | bytes 1572868
  345.5 9.6 %copy-start.10 = (bf16[256,256]{1,0:T(8,128)(2,1)S(1)}, bf16[256,256]{1,0:T(8,128)(2,1)}, u32[]{:S(2)}) copy-start(bf16[256,256]{1,0:T(8,128)(2,1)} %param.26) | copy-start | bytes 393220
  345.5 10.9 %copy-start.6 = (bf16[8,8,128,256]{3,1,2,0:T(8,128)(2,1)S(1)}, bf16[8,8,128,256]{3,1,2,0:T(8,128)(2,1)}, u32[]{:S(2)}) copy-start(bf16[8,8,128,256]{3,1,2,0:T(8,128)(2,1)} %copy.66) | copy-start | bytes 12582916
  555.6 2.4 copy-start.5
  562.2 12.8 %copy-start.12 = (f32[256,8]{0,1:T(8,128)S(1)}, f32[256,8]{0,1:T(8,128)}, u32[]{:S(2)}) copy-start(f32[256,8]{0,1:T(8,128)} %fusion.55) | copy-start | bytes 24580
  574.9 13.0 %copy-start.14 = (f32[8,128]{1,0:T(8,128)S(1)}, f32[8,128]{1,0:T(8,128)}, u32[]{:S(2)}) copy-start(f32[8,128]{1,0:T(8,128)} %copy-done.13) | copy-start | bytes 12292
  585.9 2.0 copy-start.7
  587.9 3.4 copy-start.21
  756.3 3.1 copy-start.11
Sparse Core Ops, SparseCore 0:
  591.4 164.8 all-reduce.2
where the time goes:
time: 773 us; the launch traced here: 767 us
  waiting for transfers between devices  349 us (45%)
  local copies, waits for them, and re-layouts  165 us (21%)
  matrix products  119 us (15%)
  blocking collectives  78.1 us (10%)
  starting transfers between devices  29.9 us (4%)
  between operations  14.6 us (2%)
  other arithmetic  11.7 us (2%)
    all_to_all x1, waiting for transfers between devices, local(): lax.all_to_all(outgoing, ('src', 'tgt'), split_axis=0, concat_axis=0, til...  163 us
    all_to_all x1, waiting for transfers between devices, local(): lax.all_to_all(remote_grad.reshape(peer_count, slot_cap, block_rows, feat...  107 us
    psum x1, waiting for transfers between devices, local(): lax.psum((grad_bases, local_coef + remote_coef, grad_self), ('src', 'tgt'))  79.1 us
    psum x1, blocking collectives, local(): lax.psum((grad_bases, local_coef + remote_coef, grad_self), ('src', 'tgt'))  78.1 us
    convert_element_type x3, local copies, waits for them, and re-layouts, aggregate(): aggregated = (jnp.einsum('sij,sjh->sih', adjacency, src_rows, preferred_e...  54.5 us
    unnamed x63, local copies, waits for them, and re-layouts  48.6 us
    gather x2, local copies, waits for them, and re-layouts, local(): outgoing = node_blocks[send_block[0]]  33.2 us
    dot_general x2, matrix products, aggregate(): jnp.einsum('sij,sjh->sih', adjacency, src_rows, preferred_element_type=jn...  30.2 us
  transfers between devices with their start and end apart: 3, of which 3 were waited for; matrix products, arithmetic and copies ran while one was open for 26% of the time, Pallas kernels for 0%

commit v1 on v0

v1 whole, which is shorter than its diff:
```python
import functools
import math

import jax
import jax.numpy as jnp
from jax import lax
from jax.experimental import pallas as pl
from jax.experimental.pallas import tpu as pltpu
from jax.sharding import PartitionSpec as P

MESH = pl.DeviceIdType.MESH
MIB = 1 << 20
F32 = jnp.float32
BF16 = jnp.bfloat16
SIDE = 4
CORES = 2
BLOCKS = 8
ROWS = 128
WIDTH = 256
STEP = 8
PARTS = (("x", "y", "z", 0, 48), ("y", "z", "x", 48, 48), ("z", "x", "y", 96, 32))
AXES = ("y", "z", "x")
HOPS = (1, 3, 2)
ANY = pl.BlockSpec(memory_space=pl.ANY)
VMEM = pl.BlockSpec(memory_space=pltpu.VMEM)
SMEM = pl.BlockSpec(memory_space=pltpu.SMEM)


def place():
    src, tgt = lax.axis_index("src"), lax.axis_index("tgt")
    return {"y": src // CORES, "c": src % CORES, "z": tgt // SIDE, "x": tgt % SIDE}


def device(at):
    return (at["y"] * CORES + at["c"], at["z"] * SIDE + at["x"])


def band(at):
    return (at["y"] * CORES + at["c"]) * SIDE * SIDE + at["z"] * SIDE + at["x"]


def moved(me, axis, hop):
    return {**me, axis: (me[axis] + hop) % SIDE}


def line_peers(me, axis):
    peers = []
    for hop in HOPS:
        for flip in (0, 1):
            peers.append((hop, flip, {**moved(me, axis, hop), "c": (me["c"] + flip) % CORES}))
    peers.append((0, 1, {**me, "c": (me["c"] + 1) % CORES}))
    return peers


def greet(peers):
    barrier = pltpu.get_barrier_semaphore()
    for peer in peers:
        pl.semaphore_signal(barrier, inc=1, device_id=device(peer), device_id_type=MESH)
    pl.semaphore_wait(barrier, len(peers))


def plane_dims(last):
    return tuple(a for a in AXES if a != last)


def plane_at(ref, last, **where):
    return ref.at[tuple(where.get(a, slice(None)) for a in plane_dims(last))]


def band_at(ref, last, value, core, row, rows):
    where = {"y": slice(None), "z": slice(None), "x": slice(None), last: value}
    return ref.at[where["y"], core, where["z"], where["x"], :, pl.ds(row, rows), :]


def remote(src, dst, send, recv, peer):
    return pltpu.make_async_remote_copy(
        src_ref=src, dst_ref=dst, send_sem=send, recv_sem=recv, device_id=device(peer), device_id_type=MESH
    )


def gather_kernel(feats, picks, g0, g1, g2, i0, i1, i2, own_sem, s1, r1, s2, r2):
    me = place()
    gathered, ids = (g0, g1, g2), (i0, i1, i2)
    greet([moved(me, axis, hop) for axis in AXES for hop in HOPS])
    first, rest, own = {}, [], []
    for j, (a1, a2, last, row, rows) in enumerate(PARTS):
        for u, (src, dst) in enumerate(
            ((feats.at[:, pl.ds(row, rows), :], gathered[j]), (picks, ids[j]))
        ):
            spot = plane_at(dst, last, **{a1: me[a1], a2: me[a2]})
            copy = pltpu.make_async_copy(src, spot, own_sem.at[j, u])
            copy.start()
            own.append(copy)
    for hop in HOPS:
        for j, (a1, a2, last, row, rows) in enumerate(PARTS):
            for u, (src, dst) in enumerate(
                ((feats.at[:, pl.ds(row, rows), :], gathered[j]), (picks, ids[j]))
            ):
                spot = plane_at(dst, last, **{a1: me[a1], a2: me[a2]})
                copy = remote(src, spot, s1.at[j, u, hop - 1], r1.at[j, u, hop - 1], moved(me, a1, hop))
                copy.start()
                first[j, u, hop] = copy
                copy = remote(src, spot, s2.at[j, u, 0, hop - 1], r2.at[j, u, 0, hop - 1], moved(me, a2, hop))
                copy.start()
                rest.append(copy)
    for back in HOPS:
        for j, (a1, a2, last, row, rows) in enumerate(PARTS):
            for u, dst in enumerate((gathered[j], ids[j])):
                first[j, u, back].wait_recv()
                spot = plane_at(dst, last, **{a1: (me[a1] + SIDE - back) % SIDE, a2: me[a2]})
                for hop in HOPS:
                    copy = remote(
                        spot, spot, s2.at[j, u, back, hop - 1], r2.at[j, u, back, hop - 1], moved(me, a2, hop)
                    )
                    copy.start()
                    rest.append(copy)
    for copy in own:
        copy.wait()
    for copy in first.values():
        copy.wait_send()
    for copy in rest:
        copy.wait()


def gather_plane(feats, picks):
    shapes = [jax.ShapeDtypeStruct((SIDE, SIDE, BLOCKS, rows, WIDTH), BF16) for *_, rows in PARTS]
    shapes += [jax.ShapeDtypeStruct((SIDE, SIDE) + picks.shape, jnp.int32)] * 3
    dma = pltpu.SemaphoreType.DMA
    return pl.pallas_call(
        gather_kernel,
        out_shape=shapes,
        in_specs=[ANY] * 2,
        out_specs=[ANY] * 6,
        scratch_shapes=[dma((3, 2)), dma((3, 2, 3)), dma((3, 2, 3)), dma((3, 2, 4, 3)), dma((3, 2, 4, 3))],
        compiler_params=pltpu.CompilerParams(collective_id=0, has_side_effects=True),
        name="gather_plane",
    )(feats, picks)


def exchange_kernel(g0, g1, g2, i0, i1, i2, incoming, b0, b1, b2, send, recv, own_sem):
    me = place()
    gathered, ids, packed = (g0, g1, g2), (i0, i1, i2), (b0, b1, b2)
    greet([p for axis in AXES for hop, flip, p in line_peers(me, axis) if hop] + [{**me, "c": (me["c"] + 1) % CORES}])
    copies = []

    def pack(j, slot, owner):
        def one(n, _):
            a, b = n // SIDE, n % SIDE
            for c in range(2):
                packed[j][slot, a, b, c] = gathered[j][a, b, ids[j][a, b, c, owner]]
            return 0

        lax.fori_loop(0, SIDE * SIDE, one, 0)

    for n in range(7):
        for j, (a1, a2, last, row, rows) in enumerate(PARTS):
            hop, flip, peer = line_peers(me, last)[n]
            pack(j, n, band(peer))
            copy = remote(
                packed[j].at[n],
                band_at(incoming, last, me[last], me["c"], row, rows),
                send.at[j, n],
                recv.at[j, n],
                peer,
            )
            copy.start()
            copies.append(copy)
    for j, (a1, a2, last, row, rows) in enumerate(PARTS):
        pack(j, 7, band(me))
        copy = pltpu.make_async_copy(
            packed[j].at[7], band_at(incoming, last, me[last], me["c"], row, rows), own_sem.at[j]
        )
        copy.start()
        copies.append(copy)
    for copy in copies:
        copy.wait()


def exchange_picks(gathered, ids):
    dma = pltpu.SemaphoreType.DMA
    return pl.pallas_call(
        exchange_kernel,
        out_shape=jax.ShapeDtypeStruct((SIDE, CORES, SIDE, SIDE, 2, ROWS, WIDTH), BF16),
        in_specs=[VMEM] * 3 + [SMEM] * 3,
        out_specs=ANY,
        scratch_shapes=[pltpu.VMEM((8, SIDE, SIDE, 2, rows, WIDTH), BF16) for *_, rows in PARTS]
        + [dma((3, 7)), dma((3, 7)), dma((3,))],
        compiler_params=pltpu.CompilerParams(collective_id=1, has_side_effects=True, vmem_limit_bytes=48 * MIB),
        name="exchange_picks",
    )(*gathered, *ids)


def return_kernel(grads, r0, r1, r2, send, recv, own_sem):
    me = place()
    returned = (r0, r1, r2)
    greet([p for axis in AXES for hop, flip, p in line_peers(me, axis) if hop] + [{**me, "c": (me["c"] + 1) % CORES}])
    copies = []
    for n in range(7):
        for j, (a1, a2, last, row, rows) in enumerate(PARTS):
            hop, flip, peer = line_peers(me, last)[n]
            copy = remote(
                band_at(grads, last, peer[last], peer["c"], row, rows),
                returned[j].at[me["c"], me[last]],
                send.at[j, n],
                recv.at[j, n],
                peer,
            )
            copy.start()
            copies.append(copy)
    for j, (a1, a2, last, row, rows) in enumerate(PARTS):
        copy = pltpu.make_async_copy(
            band_at(grads, last, me[last], me["c"], row, rows), returned[j].at[me["c"], me[last]], own_sem.at[j]
        )
        copy.start()
        copies.append(copy)
    for copy in copies:
        copy.wait()


def return_grads(grads):
    dma = pltpu.SemaphoreType.DMA
    return pl.pallas_call(
        return_kernel,
        out_shape=[
            jax.ShapeDtypeStruct((CORES, SIDE, SIDE, SIDE, 2, rows, WIDTH), BF16) for *_, rows in PARTS
        ],
        in_specs=[ANY],
        out_specs=[ANY] * 3,
        scratch_shapes=[dma((3, 7)), dma((3, 7)), dma((3,))],
        compiler_params=pltpu.CompilerParams(collective_id=2, has_side_effects=True),
        name="return_grads",
    )(grads)


def scatter_kernel(owners, i0, i1, i2, r0, r1, r2, p0, p1, p2, t0, t1, t2):
    ids, returned, sums, totals = (i0, i1, i2), (r0, r1, r2), (p0, p1, p2), (t0, t1, t2)
    a, b = pl.program_id(0), pl.program_id(1)
    for j in range(3):
        totals[j][...] = jnp.zeros_like(totals[j])
        for n in range(CORES * SIDE):
            for c in range(2):
                block = ids[j][a, b, c, owners[j, n]]
                totals[j][block] += returned[j][n // SIDE, n % SIDE, 0, 0, c].astype(F32)
        sums[j][0, 0] = totals[j][...].astype(BF16)


def scatter_blocks(owners, ids, returned):
    return pl.pallas_call(
        scatter_kernel,
        grid=(SIDE, SIDE),
        out_shape=[jax.ShapeDtypeStruct((SIDE, SIDE, BLOCKS, rows, WIDTH), BF16) for *_, rows in PARTS],
        in_specs=[SMEM] * 4
        + [
            pl.BlockSpec((CORES, SIDE, 1, 1, 2, rows, WIDTH), lambda a, b: (0, 0, a, b, 0, 0, 0))
            for *_, rows in PARTS
        ],
        out_specs=[pl.BlockSpec((1, 1, BLOCKS, rows, WIDTH), lambda a, b: (a, b, 0, 0, 0)) for *_, rows in PARTS],
        scratch_shapes=[pltpu.VMEM((BLOCKS, rows, WIDTH), F32) for *_, rows in PARTS],
        compiler_params=pltpu.CompilerParams(vmem_limit_bytes=32 * MIB),
        name="scatter_blocks",
    )(owners, *ids, *returned)


def reduce_kernel(p0, p1, p2, extra, out, a0, a1_, a2_, q0, q1, q2, b0, b1, b2, s1, r1, s2, r2):
    me = place()
    sums, landed, held, final = (p0, p1, p2), (a0, a1_, a2_), (q0, q1, q2), (b0, b1, b2)
    greet([moved(me, axis, hop) for axis in AXES for hop in HOPS])
    first, second = {}, {}

    def pick(j, near, far):
        a1, a2, last, row, rows = PARTS[j]
        return {a1: near, a2: far}

    for hop in HOPS:
        for j, (a1, a2, last, row, rows) in enumerate(PARTS):
            for k in range(SIDE):
                copy = remote(
                    plane_at(sums[j], last, **{a1: k, a2: (me[a2] + hop) % SIDE}),
                    landed[j].at[hop - 1, k],
                    s1.at[j, hop - 1, k],
                    r1.at[j, hop - 1, k],
                    moved(me, a2, hop),
                )
                copy.start()
                first[j, hop, k] = copy
    for j in range(3):
        for hop in HOPS:
            for k in range(SIDE):
                first[j, hop, k].wait()
    for hop in HOPS + (0,):
        for j, (a1, a2, last, row, rows) in enumerate(PARTS):
            k = (me[a1] + hop) % SIDE
            mine = plane_at(sums[j], last, **{a1: k, a2: me[a2]})

            def add(n, _, j=j, k=k, hop=hop, mine=mine):
                total = mine[n].astype(F32)
                for h in range(3):
                    total = total + landed[j][h, k, n].astype(F32)
                held[j][hop, n] = total.astype(BF16)
                return 0

            lax.fori_loop(0, BLOCKS, add, 0)
            if hop:
                copy = remote(
                    held[j].at[hop],
                    final[j].at[hop - 1],
                    s2.at[j, hop - 1],
                    r2.at[j, hop - 1],
                    moved(me, a1, hop),
                )
                copy.start()
                second[j, hop] = copy
    for copy in second.values():
        copy.wait()
    for j, (a1, a2, last, row, rows) in enumerate(PARTS):

        def end(n, _, j=j, row=row, rows=rows):
            total = extra[n, pl.ds(row, rows), :] + held[j][0, n].astype(F32)
            for h in range(3):
                total = total + final[j][h, n].astype(F32)
            out[n, pl.ds(row, rows), :] = total.astype(BF16)
            return 0

        lax.fori_loop(0, BLOCKS, end, 0)


def reduce_plane(sums, extra):
    dma = pltpu.SemaphoreType.DMA
    return pl.pallas_call(
        reduce_kernel,
        out_shape=jax.ShapeDtypeStruct((BLOCKS, ROWS, WIDTH), BF16),
        in_specs=[VMEM] * 4,
        out_specs=VMEM,
        scratch_shapes=[pltpu.VMEM((3, SIDE, BLOCKS, rows, WIDTH), BF16) for *_, rows in PARTS]
        + [pltpu.VMEM((SIDE, BLOCKS, rows, WIDTH), BF16) for *_, rows in PARTS]
        + [pltpu.VMEM((3, BLOCKS, rows, WIDTH), BF16) for *_, rows in PARTS]
        + [dma((3, 3, SIDE)), dma((3, 3, SIDE)), dma((3, 3)), dma((3, 3))],
        compiler_params=pltpu.CompilerParams(collective_id=3, has_side_effects=True, vmem_limit_bytes=48 * MIB),
        name="reduce_plane",
    )(*sums, extra)


def slot_specs(remote_steps):
    return [
        pl.BlockSpec((STEP, ROWS, ROWS), lambda i: (jnp.minimum(i, remote_steps - 1), 0, 0)),
        pl.BlockSpec((STEP, ROWS, ROWS), lambda i: (jnp.maximum(i - remote_steps, 0), 0, 0)),
    ]


def whole(shape):
    return pl.BlockSpec(shape, lambda i: (0,) * len(shape), pipeline_mode=pl.Buffered(1))


def degree_kernel(remote_steps, tgt, valid, remote_adj, local_adj, cot, scaled, norm, total):
    i = pl.program_id(0)

    @pl.when(i == 0)
    def _():
        total[...] = jnp.zeros_like(total)

    def add(adj):
        for l in range(STEP):
            s = i * STEP + l
            total[tgt[s]] += adj[l].astype(F32) * valid[s]

    @pl.when(i < remote_steps)
    def _():
        add(remote_adj)

    @pl.when(i >= remote_steps)
    def _():
        add(local_adj)

    @pl.when(i == pl.num_programs(0) - 1)
    def _():
        for t in range(BLOCKS):
            row_norm = lax.rsqrt(1.0 + jnp.sum(total[t], axis=1, keepdims=True))
            scaled[t] = (cot[t].astype(F32) * row_norm).astype(BF16)
            norm[t] = jnp.broadcast_to(row_norm, (ROWS, ROWS))


def degrees(tgt, valid, remote_adj, local_adj, cot):
    remote_steps, local_steps = remote_adj.shape[0] // STEP, local_adj.shape[0] // STEP
    return pl.pallas_call(
        functools.partial(degree_kernel, remote_steps),
        grid=(remote_steps + local_steps,),
        out_shape=[
            jax.ShapeDtypeStruct((BLOCKS, ROWS, WIDTH), BF16),
            jax.ShapeDtypeStruct((BLOCKS, ROWS, ROWS), F32),
        ],
        in_specs=[SMEM] * 2 + slot_specs(remote_steps) + [whole((BLOCKS, ROWS, WIDTH))],
        out_specs=[whole((BLOCKS, ROWS, WIDTH)), whole((BLOCKS, ROWS, ROWS))],
        scratch_shapes=[pltpu.VMEM((BLOCKS, ROWS, ROWS), F32)],
        compiler_params=pltpu.CompilerParams(vmem_limit_bytes=32 * MIB),
        name="degrees",
    )(tgt, valid, remote_adj, local_adj, cot)


def weight_kernel(coeffs, bases, scaled, weights, cots):
    r = pl.program_id(0)
    for n in range(8):
        rows = pl.ds(n * 32, 32)
        total = coeffs[r, 0] * bases[0, rows, :].astype(F32)
        for b in range(1, 8):
            total = total + coeffs[r, b] * bases[b, rows, :].astype(F32)
        weights[0, rows, :] = total.astype(BF16)
    cots[0] = lax.dot_general(
        scaled[...], weights[0], (((1,), (1,)), ((), ())), preferred_element_type=F32
    ).astype(BF16)


def mix_weights(coeffs, bases, scaled):
    relations = coeffs.shape[0]
    nodes = BLOCKS * ROWS
    return pl.pallas_call(
        weight_kernel,
        grid=(relations,),
        out_shape=[
            jax.ShapeDtypeStruct((relations, WIDTH, WIDTH), BF16),
            jax.ShapeDtypeStruct((relations, nodes, WIDTH), BF16),
        ],
        in_specs=[SMEM, whole(bases.shape), whole((nodes, WIDTH))],
        out_specs=[
            pl.BlockSpec((1, WIDTH, WIDTH), lambda r: (r, 0, 0)),
            pl.BlockSpec((1, nodes, WIDTH), lambda r: (r, 0, 0)),
        ],
        compiler_params=pltpu.CompilerParams(vmem_limit_bytes=32 * MIB),
        name="mix_weights",
    )(coeffs, bases, scaled)


def backward_kernel(remote_steps, tgt, rel, valid, src, remote_adj, local_adj, cots, cot, self_weight, grads, extra):
    i = pl.program_id(0)

    @pl.when(i == 0)
    def _():
        for t in range(BLOCKS):
            extra[t] = lax.dot_general(
                cot[t], self_weight[...], (((1,), (1,)), ((), ())), preferred_element_type=F32
            )

    def grad(adj, l):
        s = i * STEP + l
        return lax.dot_general(
            adj[l], cots[rel[s], tgt[s]], (((0,), (0,)), ((), ())), preferred_element_type=F32
        )

    @pl.when(i < remote_steps)
    def _():
        for l in range(STEP):
            grads[l] = (grad(remote_adj, l) * valid[i * STEP + l]).astype(BF16)

    @pl.when(i >= remote_steps)
    def _():
        for l in range(STEP):
            extra[src[(i - remote_steps) * STEP + l]] += grad(local_adj, l).astype(BF16).astype(F32)


def backward_slots(tgt, rel, valid, src, remote_adj, local_adj, cots, cot, self_weight):
    remote_steps, local_steps = remote_adj.shape[0] // STEP, local_adj.shape[0] // STEP
    return pl.pallas_call(
        functools.partial(backward_kernel, remote_steps),
        grid=(remote_steps + local_steps,),
        out_shape=[
            jax.ShapeDtypeStruct((remote_adj.shape[0], ROWS, WIDTH), BF16),
            jax.ShapeDtypeStruct((BLOCKS, ROWS, WIDTH), F32),
        ],
        in_specs=[SMEM] * 4
        + slot_specs(remote_steps)
        + [whole(cots.shape), whole((BLOCKS, ROWS, WIDTH)), whole((WIDTH, WIDTH))],
        out_specs=[
            pl.BlockSpec((STEP, ROWS, WIDTH), lambda i: (jnp.minimum(i, remote_steps - 1), 0, 0)),
            whole((BLOCKS, ROWS, WIDTH)),
        ],
        compiler_params=pltpu.CompilerParams(vmem_limit_bytes=48 * MIB),
        name="backward_slots",
    )(tgt, rel, valid, src, remote_adj, local_adj, cots, cot, self_weight)


def forward_kernel(
    remote_steps, tgt, rel, valid, src, coeffs, remote_adj, local_adj, incoming, feats, weights, scaled, cot, norm,
    self_weight, bases, out, terms, mixed, outer,
):
    i = pl.program_id(0)

    @pl.when(i == 0)
    def _():
        mixed[...] = jnp.zeros_like(mixed)
        outer[...] = jnp.zeros_like(outer)

    def visit(adj, rows, s):
        aggregated = (jnp.dot(adj, rows, preferred_element_type=F32) * valid[s]).astype(BF16)
        mixed[tgt[s]] += jnp.dot(aggregated, weights[rel[s]], preferred_element_type=F32)
        outer[rel[s]] += lax.dot_general(
            aggregated, scaled[tgt[s]], (((0,), (0,)), ((), ())), preferred_element_type=F32
        )

    @pl.when(i < remote_steps)
    def _():
        for l in range(STEP):
            visit(remote_adj[l], incoming[l], i * STEP + l)

    @pl.when(i >= remote_steps)
    def _():
        for l in range(STEP):
            visit(local_adj[l], feats[src[(i - remote_steps) * STEP + l]], i * STEP + l)

    @pl.when(i == pl.num_programs(0) - 1)
    def _():
        relations = outer.shape[0]
        basis_count = bases.shape[0]
        for t in range(BLOCKS):
            own = jnp.dot(feats[t], self_weight[...], preferred_element_type=F32)
            for half in range(2):
                cols = pl.ds(half * ROWS, ROWS)
                out[t, :, cols] = (
                    norm[t] * mixed[t, :, cols] + own[:, half * ROWS : (half + 1) * ROWS]
                ).astype(BF16)
        self_grad = jnp.zeros((WIDTH, WIDTH), F32)
        for t in range(BLOCKS):
            self_grad += lax.dot_general(feats[t], cot[t], (((0,), (0,)), ((), ())), preferred_element_type=F32)
        terms[pl.ds(basis_count * WIDTH, WIDTH), :] = self_grad

        def mix(n, _):
            rows = pl.ds(n * 8, 8)
            totals = [jnp.zeros((8, WIDTH), F32) for _ in range(basis_count)]
            for r in range(relations):
                piece = outer[r, rows, :]
                totals = [totals[b] + coeffs[r, b] * piece for b in range(basis_count)]
            for b in range(basis_count):
                terms[pl.ds(b * WIDTH + n * 8, 8), :] = totals[b]
            return 0

        lax.fori_loop(0, WIDTH // 8, mix, 0)

        def inner(r, _):
            def part(n, totals):
                rows = pl.ds(n * 16, 16)
                piece = outer[r, rows, :]
                return tuple(totals[b] + piece * bases[b, rows, :].astype(F32) for b in range(basis_count))

            totals = lax.fori_loop(
                0, WIDTH // 16, part, tuple(jnp.zeros((16, WIDTH), F32) for _ in range(basis_count))
            )
            rows = [jnp.sum(total, axis=0, keepdims=True) for total in totals]
            terms[pl.ds((basis_count + 1) * WIDTH + r * basis_count, basis_count), :] = jnp.concatenate(rows, axis=0)
            return 0

        lax.fori_loop(0, relations, inner, 0)


def forward_slots(
    tgt, rel, valid, src, coeffs, remote_adj, local_adj, incoming, feats, weights, scaled, cot, norm, self_weight, bases
):
    remote_steps, local_steps = remote_adj.shape[0] // STEP, local_adj.shape[0] // STEP
    relations, basis_count = coeffs.shape
    term_rows = (basis_count + 1) * WIDTH + relations * basis_count
    return pl.pallas_call(
        functools.partial(forward_kernel, remote_steps),
        grid=(remote_steps + local_steps,),
        out_shape=[
            jax.ShapeDtypeStruct((BLOCKS, ROWS, WIDTH), BF16),
            jax.ShapeDtypeStruct((term_rows, WIDTH), F32),
        ],
        in_specs=[SMEM] * 5
        + slot_specs(remote_steps)
        + [pl.BlockSpec((STEP, ROWS, WIDTH), lambda i: (jnp.minimum(i, remote_steps - 1), 0, 0))]
        + [whole(a.shape) for a in (feats, weights, scaled, cot, norm, self_weight, bases)],
        out_specs=[whole((BLOCKS, ROWS, WIDTH)), whole((term_rows, WIDTH))],
        scratch_shapes=[
            pltpu.VMEM((BLOCKS, ROWS, WIDTH), F32),
            pltpu.VMEM((relations, WIDTH, WIDTH), F32),
        ],
        compiler_params=pltpu.CompilerParams(vmem_limit_bytes=48 * MIB),
        name="forward_slots",
    )(tgt, rel, valid, src, coeffs, remote_adj, local_adj, incoming, feats, weights, scaled, cot, norm, self_weight, bases)


def local(
    node_feats, send_block, recv_block, recv_rel, recv_count, recv_adj, local_src, local_tgt, local_rel, local_adj,
    bases, coeffs, self_weight, cotangent,
):
    peers = lax.axis_size(("src", "tgt"))
    slot_cap = send_block.shape[2]
    remote_slots = peers * slot_cap
    relations, basis_count = coeffs.shape
    feats = node_feats.reshape(BLOCKS, ROWS, WIDTH)
    cot = cotangent.reshape(BLOCKS, ROWS, WIDTH)
    me = place()
    gathered_ids = gather_plane(feats, send_block[0].T)
    gathered, ids = gathered_ids[:3], gathered_ids[3:]
    incoming = exchange_picks(gathered, ids).reshape(remote_slots, ROWS, WIDTH)

    remote_adj = recv_adj.reshape(remote_slots, ROWS, ROWS)
    own_adj = local_adj[0]
    src = local_src[0]
    tgt = jnp.concatenate([recv_block.reshape(remote_slots), local_tgt[0]])
    rel = jnp.concatenate([recv_rel.reshape(remote_slots), local_rel[0]])
    remote_valid = (jnp.arange(slot_cap, dtype=jnp.int32)[None, :] < recv_count[0][:, None]).astype(F32)
    valid = jnp.concatenate([remote_valid.reshape(remote_slots), jnp.ones((src.shape[0],), F32)])
    wide_coeffs = coeffs.astype(F32)
    scaled, norm = degrees(tgt, valid, remote_adj, own_adj, cot)
    weights, cots = mix_weights(wide_coeffs, bases, scaled.reshape(BLOCKS * ROWS, WIDTH))
    cots = cots.reshape(relations, BLOCKS, ROWS, WIDTH)
    grads, extra = backward_slots(tgt, rel, valid, src, remote_adj, own_adj, cots, cot, self_weight)
    features_out, terms = forward_slots(
        tgt, rel, valid, src, wide_coeffs, remote_adj, own_adj, incoming, feats, weights, scaled, cot, norm,
        self_weight, bases,
    )
    totals = lax.psum(terms, ("src", "tgt"))
    returned = return_grads(grads.reshape(SIDE, CORES, SIDE, SIDE, slot_cap, ROWS, WIDTH))
    owners = jnp.stack(
        [
            jnp.stack([band({**me, "c": core, last: k}) for core in range(CORES) for k in range(SIDE)])
            for _, _, last, _, _ in PARTS
        ]
    ).astype(jnp.int32)
    sums = scatter_blocks(owners, ids, returned)
    grad_features = reduce_plane(sums, extra)
    totals = totals * (1.0 / math.sqrt(node_feats.shape[0] * peers))
    basis_rows = basis_count * WIDTH
    return (
        features_out.reshape(node_feats.shape),
        grad_features.reshape(node_feats.shape),
        totals[:basis_rows].reshape(basis_count, WIDTH, WIDTH),
        jnp.sum(totals[basis_rows + WIDTH :], axis=1).reshape(relations, basis_count),
        totals[basis_rows : basis_rows + WIDTH],
    )


def solution(mesh):
    both = ("src", "tgt")
    in_specs = (
        P(both, None),
        P(both, None, None),
        P(both, None, None),
        P(both, None, None),
        P(both, None),
        P(both, None, None, None, None),
        P(both, None),
        P(both, None),
        P(both, None),
        P(both, None, None, None),
        P(),
        P(),
        P(),
        P(both, None),
    )
    out_specs = (P(both, None), P(both, None), P(), P(), P())
    return jax.shard_map(local, mesh=mesh, in_specs=in_specs, out_specs=out_specs, check_vma=False)
```

time: 773 us -> 463 us (0.60)
  Pallas kernels: 0 us -> 414 us
  waiting for transfers between devices: 349 us -> 0.04 us
  local copies, waits for them, and re-layouts: 165 us -> 29.4 us
  matrix products: 119 us -> 0 us
  blocking collectives: 78.1 us -> 0 us
  starting transfers between devices: 29.9 us -> 0.04 us
  other arithmetic: 11.7 us -> 3.52 us
    pallas_call x0 -> x9, Pallas kernels: none -> 414 us  [the longest x1 86.1 us: forward_slots(): pl.pallas_call(functools.partial(forward_kernel, remote_steps), grid=(rem...]
    all_to_all x2 -> x0, waiting for transfers between devices: 270 us -> none  [the longest x1 163 us: local(): lax.all_to_all(outgoing, ('src', 'tgt'), split_axis=0, concat_axis=0, til...]
    dot_general x24 -> x0, matrix products: 119 us -> none  [the longest x2 30.2 us: aggregate(): jnp.einsum('sij,sjh->sih', adjacency, src_rows, preferred_element_type=jn...]
    psum x1, waiting for transfers between devices: 79.1 us -> 0.02 us  [local(): totals = lax.psum(terms, ('src', 'tgt'))]
    psum x1 -> x0, blocking collectives: 78.1 us -> none  [local(): lax.psum((grad_bases, local_coef + remote_coef, grad_self), ('src', 'tgt'))]
    convert_element_type x4 -> x1, local copies, waits for them, and re-layouts: 54.6 us -> 0.15 us  [local(): (jnp.arange(slot_cap, dtype=jnp.int32)[None, :] < recv_count[0][:, None])...]
    gather x3 -> x0, local copies, waits for them, and re-layouts: 36 us -> none  [the longest x2 33.2 us: local(): outgoing = node_blocks[send_block[0]]]
    all_to_all x2 -> x0, starting transfers between devices: 29.9 us -> none  [the longest x1 17.2 us: local(): lax.all_to_all(remote_grad.reshape(peer_count, slot_cap, block_rows, feat...]
  transfers between devices with their start and end apart: 3 -> 1, of which waited for: 3 -> 0; matrix products, arithmetic and copies ran while one was open for 26% -> 0% of each run, Pallas kernels for 0% -> 39%
where the time goes in v1:
time: 463 us; the launch traced here: 462 us
  Pallas kernels  414 us (89%)
  local copies, waits for them, and re-layouts  29.4 us (6%)
  between operations  14.3 us (3%)
    pallas_call x1, Pallas kernels, forward_slots(): pl.pallas_call(functools.partial(forward_kernel, remote_steps), grid=(rem...  86.1 us
    pallas_call x1, Pallas kernels, exchange_picks(): pl.pallas_call(exchange_kernel, out_shape=jax.ShapeDtypeStruct((SIDE, COR...  77.3 us
    pallas_call x1, Pallas kernels, return_grads(): pl.pallas_call(return_kernel, out_shape=[jax.ShapeDtypeStruct((CORES, SID...  75.4 us
    pallas_call x1, Pallas kernels, reduce_plane(): pl.pallas_call(reduce_kernel, out_shape=jax.ShapeDtypeStruct((BLOCKS, ROW...  56.5 us
    pallas_call x1, Pallas kernels, gather_plane(): pl.pallas_call(gather_kernel, out_shape=shapes, in_specs=[ANY] * 2, out_s...  52.3 us
    pallas_call x1, Pallas kernels, backward_slots(): pl.pallas_call(functools.partial(backward_kernel, remote_steps), grid=(re...  34 us
    unnamed x49, local copies, waits for them, and re-layouts  26.5 us
    pallas_call x1, Pallas kernels, mix_weights(): pl.pallas_call(weight_kernel, grid=(relations,), out_shape=[jax.ShapeDtyp...  15.6 us
  transfers between devices with their start and end apart: 1, of which 0 were waited for; matrix products, arithmetic and copies ran while one was open for 0% of the time, Pallas kernels for 39%

profile of v1, /device:TPU:1, one launch (start us, length us, event | category | flops | bytes accessed | tf_op | source)
XLA Modules:
  0.0 461.8 jit_solution(6108984343938794913)
XLA Ops:
  7.2 0.8 copy.20
  8.0 0.1 reshape.56
  8.1 0.8 copy.21
  8.9 0.1 reshape.57
  9.1 0.7 iota_compare_fusion
  9.8 0.1 convert_element_type.8
  10.0 0.8 copy.22
  10.8 52.3 %gather_plane.1 = (bf16[4,4,8,48,256]{4,3,2,1,0:T(8,128)(2,1)}, bf16[4,4,8,48,256]{4,3,2,1,0:T(8,128)(2,1)}, bf16[4,4,8,32,256]{4,3,2,1,0:T(8,128)(2,1)}, s32[4,...) custom-call(bf16[8,128,256]{2,1,0:T(8,128)(2,1)} %bitcast.56, s32[2,128]{1,0:T(2,128)} %bitcast.67), custom_call_target="tpu_custom_call" | custom-call | tf_op jit(solution)/shard_map/gather_plane/pallas_call | solution.py:129
  63.0 0.7 pad_add_fusion
  63.7 3.4 copy-done
  67.1 1.6 copy-done.1
  68.7 1.0 copy-done.5
  69.8 5.0 %degrees.1 = (bf16[8,128,256]{2,1,0:T(8,128)(2,1)S(1)}, f32[8,128,128]{2,1,0:T(8,128)S(1)}) custom-call(s32[320]{0:T(512)S(1)} %get-tuple-element.50.tgt, f32[320]{0:T(512)S(1)} %pad_convert_fusion.valid, bf16[256,128,128]{2,1,0:T(8,128)(2,1)S(1)} %bitcast.47, bf16[64,128,128]{2,1,0:T(8,128)(2,1)S(1)} %bitcast.48, bf16[8,128,256]{2,1,0:T(8,128)(2,1)S(1)} %bitcast.52), custom_call_target="tpu_custom_call" | custom-call | tf_op jit(solution)/shard_map/degrees/pallas_call | solution.py:384
  74.8 15.6 %mix_weights.1 = (bf16[30,256,256]{2,1,0:T(8,128)(2,1)S(1)}, bf16[30,1024,256]{2,1,0:T(8,128)(2,1)S(1)}) custom-call(f32[30,8]{1,0:T(8,128)S(1)} %convert_element_type.9.coeffs, bf16[8,256,256]{2,1,0:T(8,128)(2,1)S(1)} %copy-done.8, bf16[1024,256]{1,0:T(8,128)(2,1)S(1)} %bitcast.55), custom_call_target="tpu_custom_call" | custom-call | tf_op jit(solution)/shard_map/mix_weights/pallas_call | solution.py:415
  90.4 5.5 %copy-done.3 = bf16[30,1024,256]{2,1,0:T(8,128)(2,1)} copy-done((bf16[30,1024,256]{2,1,0:T(8,128)(2,1)}, bf16[30,1024,256]{2,1,0:T(8,128)(2,1)S(1)}, u32[]{:S(2)}) %copy-start.3) | copy-done | bytes 15728664
  95.9 1.9 copy-done.9
  97.9 77.3 %exchange_picks.1 = bf16[4,2,4,4,2,128,256]{6,5,4,3,2,1,0:T(8,128)(2,1)} custom-call(bf16[4,4,8,48,256]{4,3,2,1,0:T(8,128)(2,1)S(1)} %copy-done.12, bf16[4,4,8,48,256]{4,3,2,1,0:T(8,128)(2,1)} %get-tuple-element.26.g1, bf16[4,4,8,32,256]{4,3,2,1,0:T(8,128)(2,1)S(1)} %copy-done.14, s32[4,4,2,128]{3,2,1,0:T(2,128)S(1)} %copy-done.18, ...), custom_call_target="tpu_custom_call" | custom-call | tf_op jit(solution)/shard_map/exchange_picks/pallas_call | solution.py:181
  175.2 86.1 %forward_slots.1 = (bf16[8,128,256]{2,1,0:T(8,128)(2,1)}, f32[2544,256]{1,0:T(8,128)}) custom-call(s32[320]{0:T(512)S(1)} %get-tuple-element.50.tgt, s32[320]{0:T(512)S(1)} %get-tuple-element.51.rel, f32[320]{0:T(512)S(1)} %pad_convert_fusion.valid, s32[64]{0:T(128)S(1)} %bitcast.59, f32[30,8]{1,0:T(8,128)S(1)} %convert_element_type.9.coeffs, ...), custom_call_target="tpu_custom_call" | custom-call | tf_op jit(solution)/shard_map/forward_slots/pallas_call | solution.py:558
  261.4 34.0 %backward_slots.1 = (bf16[256,128,256]{2,1,0:T(8,128)(2,1)}, f32[8,128,256]{2,1,0:T(8,128)S(1)}) custom-call(s32[320]{0:T(512)S(1)} %get-tuple-element.50.tgt, s32[320]{0:T(512)S(1)} %get-tuple-element.51.rel, f32[320]{0:T(512)S(1)} %pad_convert_fusion.valid, s32[64]{0:T(128)S(1)} %bitcast.60, bf16[256,128,128]{2,1,0:T(8,128)(2,1)} %bitcast.46, ...), custom_call_target="tpu_custom_call" | custom-call | tf_op jit(solution)/shard_map/backward_slots/pallas_call | solution.py:461
  295.5 1.0 copy-done.15
  296.4 75.4 %return_grads.1 = (bf16[2,4,4,4,2,48,256]{6,5,4,3,2,1,0:T(8,128)(2,1)}, bf16[2,4,4,4,2,48,256]{6,5,4,3,2,1,0:T(8,128)(2,1)}, bf16[2,4,4,4,2,32,256]{6,5,4,3,2,1,0:T(8,128)(2,1)}) custom-call(bf16[4,2,4,4,2,128,256]{6,5,4,3,2,1,0:T(8,128)(2,1)} %bitcast.62), custom_call_target="tpu_custom_call" | custom-call | tf_op jit(solution)/shard_map/return_grads/pallas_call | solution.py:222
  372.2 2.8 copy-done.4
  374.9 2.2 copy-done.7
  377.1 12.2 %scatter_blocks.1 = (bf16[4,4,8,48,256]{4,3,2,1,0:T(8,128)(2,1)S(1)}, bf16[4,4,8,48,256]{4,3,2,1,0:T(8,128)(2,1)S(1)}, bf16[4,4,8,32,256]{4,3,2,1,0:T(8,128)(2,1)S(1)}) custom-call(s32[3,8]{1,0:T(4,128)S(1)} %pad_add_fusion.2.owners, s32[4,4,2,128]{3,2,1,0:T(2,128)S(1)} %copy-done.18, s32[4,4,2,128]{3,2,1,0:T(2,128)S(1)} %copy-done.19, ...), custom_call_target="tpu_custom_call" | custom-call | tf_op jit(solution)/shard_map/scatter_blocks/pallas_call | solution.py:248
  389.4 1.6 copy-done.10
  391.0 1.7 copy-done.11
  392.7 56.5 %reduce_plane.1 = bf16[8,128,256]{2,1,0:T(8,128)(2,1)S(1)} custom-call(bf16[4,4,8,48,256]{4,3,2,1,0:T(8,128)(2,1)} %copy-done.10, bf16[4,4,8,48,256]{4,3,2,1,0:T(8,128)(2,1)} %copy-done.11, bf16[4,4,8,32,256]{4,3,2,1,0:T(8,128)(2,1)S(1)} %get-tuple-element.42.p2, f32[8,128,256]{2,1,0:T(8,128)S(1)} %copy-done.16), custom_call_target="tpu_custom_call" | custom-call | tf_op jit(solution)/shard_map/reduce_plane/pallas_call | solution.py:329
  449.2 2.0 broadcast_multiply_fusion
  451.1 1.5 slice.12
  452.6 0.7 slice.14
  453.5 0.7 copy.23
  454.2 0.8 copy.26
  (45 shorter events, 0.6 us)
Async XLA Ops:
  7.2 442.0 %all-reduce.3.cloned.1.call-start = ((), (), s32[]{:S(2)}) async-start(), calls=%async_computation | async-start | bytes 5210112 | tf_op jit(solution)/shard_map/psum | solution.py:610
  63.7 3.4 copy-start
  67.1 1.6 copy-start.1
  68.7 1.0 copy-start.5
  69.7 5.1 %copy-start.8 = (bf16[8,256,256]{2,1,0:T(8,128)(2,1)S(1)}, bf16[8,256,256]{2,1,0:T(8,128)(2,1)}, u32[]{:S(2)}) copy-start(bf16[8,256,256]{2,1,0:T(8,128)(2,1)} %bases.3) | copy-start | bytes 3145732
  69.7 28.0 %copy-start.12 = (bf16[4,4,8,48,256]{4,3,2,1,0:T(8,128)(2,1)S(1)}, bf16[4,4,8,48,256]{4,3,2,1,0:T(8,128)(2,1)}, u32[]{:S(2)}) copy-start(bf16[4,4,8,48,256]{4,3,2,1,0:T(8,128)(2,1)} %get-tuple-element.25.g0) | copy-start | bytes 9437188
  69.7 28.0 %copy-start.14 = (bf16[4,4,8,32,256]{4,3,2,1,0:T(8,128)(2,1)S(1)}, bf16[4,4,8,32,256]{4,3,2,1,0:T(8,128)(2,1)}, u32[]{:S(2)}) copy-start(bf16[4,4,8,32,256]{4,3,2,1,0:T(8,128)(2,1)} %get-tuple-element.27.g2) | copy-start | bytes 6291460
  69.7 28.0 %copy-start.18 = (s32[4,4,2,128]{3,2,1,0:T(2,128)S(1)}, s32[4,4,2,128]{3,2,1,0:T(2,128)}, u32[]{:S(2)}) copy-start(s32[4,4,2,128]{3,2,1,0:T(2,128)} %get-tuple-element.28.i0) | copy-start | bytes 49156
  69.7 28.0 %copy-start.19 = (s32[4,4,2,128]{3,2,1,0:T(2,128)S(1)}, s32[4,4,2,128]{3,2,1,0:T(2,128)}, u32[]{:S(2)}) copy-start(s32[4,4,2,128]{3,2,1,0:T(2,128)} %get-tuple-element.29.i1) | copy-start | bytes 49156
  69.8 28.0 %copy-start.20 = (s32[4,4,2,128]{3,2,1,0:T(2,128)S(1)}, s32[4,4,2,128]{3,2,1,0:T(2,128)}, u32[]{:S(2)}) copy-start(s32[4,4,2,128]{3,2,1,0:T(2,128)} %get-tuple-element.30.i2) | copy-start | bytes 49156
  90.4 5.5 %copy-start.3 = (bf16[30,1024,256]{2,1,0:T(8,128)(2,1)}, bf16[30,1024,256]{2,1,0:T(8,128)(2,1)S(1)}, u32[]{:S(2)}) copy-start(bf16[30,1024,256]{2,1,0:T(8,128)(2,1)S(1)} %get-tuple-element.35) | copy-start | bytes 47185924
  95.9 1.9 copy-start.9
  97.8 77.4 %copy-start.2 = (bf16[1,64,128,128]{3,2,1,0:T(8,128)(2,1)S(1)}, bf16[1,64,128,128]{3,2,1,0:T(8,128)(2,1)}, u32[]{:S(2)}) copy-start(bf16[1,64,128,128]{3,2,1,0:T(8,128)(2,1)} %param.23) | copy-start | bytes 6291460
  97.8 77.4 %copy-start.6 = (bf16[1024,256]{1,0:T(8,128)(2,1)S(1)}, bf16[1024,256]{1,0:T(8,128)(2,1)}, u32[]{:S(2)}) copy-start(bf16[1024,256]{1,0:T(8,128)(2,1)} %param.27) | copy-start | bytes 1572868
  97.8 77.4 %copy-start.13 = (bf16[1024,256]{1,0:T(8,128)(2,1)S(1)}, bf16[1024,256]{1,0:T(8,128)(2,1)}, u32[]{:S(2)}) copy-start(bf16[1024,256]{1,0:T(8,128)(2,1)} %param.14) | copy-start | bytes 1572868
  97.8 77.4 %copy-start.17 = (bf16[256,256]{1,0:T(8,128)(2,1)S(1)}, bf16[256,256]{1,0:T(8,128)(2,1)}, u32[]{:S(2)}) copy-start(bf16[256,256]{1,0:T(8,128)(2,1)} %self_weight.3) | copy-start | bytes 393220
  97.8 77.4 %copy-start.21 = (s32[1,64]{1,0:T(1,128)S(1)}, s32[1,64]{1,0:T(1,128)}, u32[]{:S(2)}) copy-start(s32[1,64]{1,0:T(1,128)} %param.20) | copy-start | bytes 772
  295.5 1.0 copy-start.15
  372.1 2.8 copy-start.4
  374.9 2.2 copy-start.7
  377.1 15.6 %copy-start.16 = (f32[8,128,256]{2,1,0:T(8,128)S(1)}, f32[8,128,256]{2,1,0:T(8,128)}, u32[]{:S(2)}) copy-start(f32[8,128,256]{2,1,0:T(8,128)} %copy-done.15) | copy-start | bytes 3145732
  389.4 1.6 copy-start.10
  391.0 1.7 copy-start.11
Sparse Core Ops, SparseCore 0:
  261.5 175.7 all-reduce.2

commit v2 on v1

v2 whole, which is shorter than its diff:
```python
import functools
import math

import jax
import jax.numpy as jnp
from jax import lax
from jax.experimental import pallas as pl
from jax.experimental.pallas import tpu as pltpu
from jax.sharding import PartitionSpec as P

MESH = pl.DeviceIdType.MESH
MIB = 1 << 20
F32 = jnp.float32
BF16 = jnp.bfloat16
SIDE = 4
CORES = 2
BLOCKS = 8
ROWS = 128
WIDTH = 256
STEP = 8
WIDE = 32
CHUNKS = 8
TERM_ROWS = 8
TERMS = CORES * 3 * SIDE**3 * TERM_ROWS
PARTS = (("x", "y", "z", 0, 48), ("y", "z", "x", 48, 48), ("z", "x", "y", 96, 32))
AXES = ("y", "z", "x")
HOPS = (1, 3, 2)
ANY = pl.BlockSpec(memory_space=pl.ANY)
VMEM = pl.BlockSpec(memory_space=pltpu.VMEM)
SMEM = pl.BlockSpec(memory_space=pltpu.SMEM)


def place():
    src, tgt = lax.axis_index("src"), lax.axis_index("tgt")
    return {"y": src // CORES, "c": src % CORES, "z": tgt // SIDE, "x": tgt % SIDE}


def device(at):
    return (at["y"] * CORES + at["c"], at["z"] * SIDE + at["x"])


def band(at):
    return (at["y"] * CORES + at["c"]) * SIDE * SIDE + at["z"] * SIDE + at["x"]


def moved(me, axis, hop):
    return {**me, axis: (me[axis] + hop) % SIDE}


def line_peers(me, axis):
    peers = []
    for hop in HOPS:
        for flip in (0, 1):
            peers.append((hop, flip, {**moved(me, axis, hop), "c": (me["c"] + flip) % CORES}))
    peers.append((0, 1, {**me, "c": (me["c"] + 1) % CORES}))
    return peers


def greet(peers):
    barrier = pltpu.get_barrier_semaphore()
    for peer in peers:
        pl.semaphore_signal(barrier, inc=1, device_id=device(peer), device_id_type=MESH)
    pl.semaphore_wait(barrier, len(peers))


def plane_dims(last):
    return tuple(a for a in AXES if a != last)


def plane_at(ref, last, **where):
    return ref.at[tuple(where.get(a, slice(None)) for a in plane_dims(last))]


def band_at(ref, core, row, rows, **where):
    where = {"y": slice(None), "z": slice(None), "x": slice(None), **where}
    return ref.at[where["y"], core, where["z"], where["x"], :, pl.ds(row, rows), :]


def remote(src, dst, send, recv, peer):
    return pltpu.make_async_remote_copy(
        src_ref=src, dst_ref=dst, send_sem=send, recv_sem=recv, device_id=device(peer), device_id_type=MESH
    )


def gather_kernel(
    coeffs, tgt, rel, valid, src, feats, picks, bases, scaled, cot, self_weight, remote_adj, local_adj,
    g0, g1, g2, i0, i1, i2, weights, extra, grads,
    adj, own_adj, cots, staged, part, own_sem, s1, r1, s2, r2, adj_sem, out_sem,
):
    me = place()
    gathered, ids = (g0, g1, g2), (i0, i1, i2)
    relations, remote_slots, local_slots = cots.shape[0], adj.shape[0], own_adj.shape[0]
    chunk = remote_slots // CHUNKS
    adj_copies = [
        pltpu.make_async_copy(remote_adj, adj, adj_sem.at[0]),
        pltpu.make_async_copy(local_adj, own_adj, adj_sem.at[1]),
    ]
    for copy in adj_copies:
        copy.start()
    greet([moved(me, axis, hop) for axis in AXES for hop in HOPS])
    first, rest, own = {}, [], []
    jobs = [
        (j, u, a1, a2, last, from_, to)
        for j, (a1, a2, last, row, rows) in enumerate(PARTS)
        for u, (from_, to) in enumerate(((feats.at[:, pl.ds(row, rows), :], gathered[j]), (picks, ids[j])))
    ]
    for hop in HOPS:
        for j, u, a1, a2, last, from_, to in jobs:
            spot = plane_at(to, last, **{a1: me[a1], a2: me[a2]})
            copy = remote(from_, spot, s1.at[j, u, hop - 1], r1.at[j, u, hop - 1], moved(me, a1, hop))
            copy.start()
            first[j, u, hop] = copy
    for hop in HOPS:
        for j, u, a1, a2, last, from_, to in jobs:
            spot = plane_at(to, last, **{a1: me[a1], a2: me[a2]})
            copy = remote(from_, spot, s2.at[j, u, 0, hop - 1], r2.at[j, u, 0, hop - 1], moved(me, a2, hop))
            copy.start()
            rest.append(copy)
    for j, u, a1, a2, last, from_, to in jobs:
        spot = plane_at(to, last, **{a1: me[a1], a2: me[a2]})
        copy = pltpu.make_async_copy(from_, spot, own_sem.at[j, u])
        copy.start()
        own.append(copy)

    def mix(r, _):
        for n in range(8):
            rows = pl.ds(n * 32, 32)
            total = coeffs[r, 0] * bases[0, rows, :].astype(F32)
            for b in range(1, 8):
                total = total + coeffs[r, b] * bases[b, rows, :].astype(F32)
            weights[r, rows, :] = total.astype(BF16)
        for t in range(BLOCKS):
            cots[r, t] = lax.dot_general(
                scaled[t], weights[r], (((1,), (1,)), ((), ())), preferred_element_type=F32
            ).astype(BF16)
        return 0

    third = relations // 3
    for n, back in enumerate(HOPS):
        lax.fori_loop(n * third, (n + 1) * third if n < 2 else relations, mix, 0)
        for j, u, a1, a2, last, from_, to in jobs:
            first[j, u, back].wait_recv()
            spot = plane_at(to, last, **{a1: (me[a1] + SIDE - back) % SIDE, a2: me[a2]})
            for hop in HOPS:
                copy = remote(spot, spot, s2.at[j, u, back, hop - 1], r2.at[j, u, back, hop - 1], moved(me, a2, hop))
                copy.start()
                rest.append(copy)

    for copy in adj_copies:
        copy.wait()

    def slot_chunk(k):
        return pltpu.make_async_copy(
            staged.at[pl.ds(k * chunk, chunk)], grads.at[pl.ds(k * chunk, chunk)], out_sem.at[k]
        )

    def remote_chunk(k, _):
        def group(g, _):
            for l in range(STEP):
                s = k * chunk + g * STEP + l
                grad = lax.dot_general(
                    adj[s], cots[rel[s], tgt[s]], (((0,), (0,)), ((), ())), preferred_element_type=F32
                )
                staged[s] = (grad * valid[s]).astype(BF16)
            return 0

        lax.fori_loop(0, chunk // STEP, group, 0)
        slot_chunk(k).start()
        return 0

    lax.fori_loop(0, CHUNKS, remote_chunk, 0)
    for t in range(BLOCKS):
        extra[t] = lax.dot_general(cot[t], self_weight[...], (((1,), (1,)), ((), ())), preferred_element_type=F32)

    def local_group(g, _):
        for l in range(STEP):
            s = remote_slots + g * STEP + l
            part[l] = lax.dot_general(
                own_adj[g * STEP + l], cots[rel[s], tgt[s]], (((0,), (0,)), ((), ())), preferred_element_type=F32
            ).astype(BF16)
        for k in range(BLOCKS):
            hits = [(src[g * STEP + l] == k).astype(F32) for l in range(STEP)]
            for n in range(4):
                rows = pl.ds(n * 32, 32)
                total = extra[k, rows, :]
                for l in range(STEP):
                    total = total + hits[l] * part[l, rows, :].astype(F32)
                extra[k, rows, :] = total
        return 0

    lax.fori_loop(0, local_slots // STEP, local_group, 0)

    def end_chunk(k, _):
        slot_chunk(k).wait()
        return 0

    lax.fori_loop(0, CHUNKS, end_chunk, 0)
    for copy in own:
        copy.wait()
    for copy in first.values():
        copy.wait_send()
    for copy in rest:
        copy.wait()


def gather_plane(coeffs, tgt, rel, valid, src, feats, picks, bases, scaled, cot, self_weight, remote_adj, local_adj):
    relations, remote_slots = coeffs.shape[0], remote_adj.shape[0]
    shapes = [jax.ShapeDtypeStruct((SIDE, SIDE, BLOCKS, rows, WIDTH), BF16) for *_, rows in PARTS]
    shapes += [jax.ShapeDtypeStruct((SIDE, SIDE) + picks.shape, jnp.int32)] * 3
    shapes += [
        jax.ShapeDtypeStruct((relations, WIDTH, WIDTH), BF16),
        jax.ShapeDtypeStruct((BLOCKS, ROWS, WIDTH), F32),
        jax.ShapeDtypeStruct((remote_slots, ROWS, WIDTH), BF16),
    ]
    dma = pltpu.SemaphoreType.DMA
    return pl.pallas_call(
        gather_kernel,
        out_shape=shapes,
        in_specs=[SMEM] * 5 + [ANY] * 2 + [VMEM] * 4 + [ANY] * 2,
        out_specs=[ANY] * 6 + [VMEM] * 2 + [ANY],
        scratch_shapes=[
            pltpu.VMEM(remote_adj.shape, BF16),
            pltpu.VMEM(local_adj.shape, BF16),
            pltpu.VMEM((relations, BLOCKS, ROWS, WIDTH), BF16),
            pltpu.VMEM((remote_slots, ROWS, WIDTH), BF16),
            pltpu.VMEM((STEP, ROWS, WIDTH), BF16),
            dma((3, 2)), dma((3, 2, 3)), dma((3, 2, 3)), dma((3, 2, 4, 3)), dma((3, 2, 4, 3)),
            dma((2,)), dma((CHUNKS,)),
        ],
        compiler_params=pltpu.CompilerParams(collective_id=0, has_side_effects=True, vmem_limit_bytes=58 * MIB),
        name="gather_plane",
    )(coeffs, tgt, rel, valid, src, feats, picks, bases, scaled, cot, self_weight, remote_adj, local_adj)


def exchange_kernel(g0, g1, g2, i0, i1, i2, incoming, b0, b1, b2, send, recv, own_sem):
    me = place()
    gathered, ids, packed = (g0, g1, g2), (i0, i1, i2), (b0, b1, b2)
    greet([p for axis in AXES for hop, flip, p in line_peers(me, axis) if hop] + [{**me, "c": (me["c"] + 1) % CORES}])
    copies = []

    def pack(j, slot, owner):
        def one(n, _):
            a, b = n // SIDE, n % SIDE
            for c in range(2):
                packed[j][slot, a, b, c] = gathered[j][a, b, ids[j][a, b, c, owner]]
            return 0

        lax.fori_loop(0, SIDE * SIDE, one, 0)

    for n in range(7):
        for j, (a1, a2, last, row, rows) in enumerate(PARTS):
            hop, flip, peer = line_peers(me, last)[n]
            pack(j, n, band(peer))
            copy = remote(
                packed[j].at[n],
                band_at(incoming, me["c"], row, rows, **{last: me[last]}),
                send.at[j, n],
                recv.at[j, n],
                peer,
            )
            copy.start()
            copies.append(copy)
    for j, (a1, a2, last, row, rows) in enumerate(PARTS):
        pack(j, 7, band(me))
        copy = pltpu.make_async_copy(
            packed[j].at[7], band_at(incoming, me["c"], row, rows, **{last: me[last]}), own_sem.at[j]
        )
        copy.start()
        copies.append(copy)
    for copy in copies:
        copy.wait()


def exchange_picks(gathered, ids):
    dma = pltpu.SemaphoreType.DMA
    return pl.pallas_call(
        exchange_kernel,
        out_shape=jax.ShapeDtypeStruct((SIDE, CORES, SIDE, SIDE, 2, ROWS, WIDTH), BF16),
        in_specs=[VMEM] * 3 + [SMEM] * 3,
        out_specs=ANY,
        scratch_shapes=[pltpu.VMEM((8, SIDE, SIDE, 2, rows, WIDTH), BF16) for *_, rows in PARTS]
        + [dma((3, 7)), dma((3, 7)), dma((3,))],
        compiler_params=pltpu.CompilerParams(collective_id=1, has_side_effects=True, vmem_limit_bytes=48 * MIB),
        name="exchange_picks",
    )(*gathered, *ids)


def return_kernel(
    scale, i0, i1, i2, grads, extra, terms, out, full,
    r0, r1, r2, p0, p1, p2, l0, l1, l2, q0, q1, q2, f0, f1, f2, added, h0, b0, h1, b1, h2, b2, b3,
    send, recv, own_sem, s1, v1, s2, v2, pair_sem, ws, wr,
):
    me = place()
    ids, returned, sums, landed = (i0, i1, i2), (r0, r1, r2), (p0, p1, p2), (l0, l1, l2)
    held, final = (q0, q1, q2), (f0, f1, f2)
    core, partner = me["c"], {**me, "c": (me["c"] + 1) % CORES}
    own = [
        pltpu.make_async_copy(terms.at[core], h0, own_sem.at[3]),
        pltpu.make_async_copy(extra, added, own_sem.at[4]),
    ]
    for j, (a1, a2, last, row, rows) in enumerate(PARTS):
        own.append(
            pltpu.make_async_copy(
                band_at(grads, core, row, rows, **{last: me[last]}), returned[j].at[core, me[last]], own_sem.at[j]
            )
        )
    for copy in own:
        copy.start()
    greet([p for axis in AXES for hop, flip, p in line_peers(me, axis) if hop] + [partner])
    halves = remote(terms.at[partner["c"]], b0, pair_sem.at[0], pair_sem.at[1], partner)
    halves.start()
    sent = [[], [], [], []]

    def give(group):
        for n in range(7):
            for j, (a1, a2, last, row, rows) in enumerate(PARTS):
                hop, flip, peer = line_peers(me, last)[n]
                far = (me[a2] + group) % SIDE
                copy = remote(
                    band_at(grads, peer["c"], row, rows, **{last: peer[last], a2: far}),
                    plane_at(returned[j].at[core, me[last]], last, **{a2: far}),
                    send.at[j, n, group],
                    recv.at[j, n, group],
                    peer,
                )
                copy.start()
                sent[group].append(copy)

    def weigh(stage, level, src, dst):
        copies = []
        for hop in HOPS:
            for j, part in enumerate(PARTS):
                axis = part[level]
                copy = remote(
                    src(j, (me[axis] + hop) % SIDE),
                    dst(j, hop - 1),
                    ws.at[stage, j, hop - 1],
                    wr.at[stage, j, hop - 1],
                    moved(me, axis, hop),
                )
                copy.start()
                copies.append(copy)
        return copies

    def done(copies):
        for copy in copies:
            copy.wait()

    def piece(j, depth):
        spot = (core, j) + tuple(me[PARTS[j][level]] for level in (2, 1, 0)[:depth])
        return full.at[spot]

    def fold(j, hop, k):
        a1, a2, last, row, rows = PARTS[j]
        where = {a1: k, a2: (me[a2] + hop) % SIDE}
        spot = tuple(where[a] for a in plane_dims(last))

        def two(n, _):
            totals = [jnp.zeros((rows, WIDTH), F32)] * 2
            for other in range(CORES):
                for place_on in range(SIDE):
                    owner = band({**me, "c": other, last: place_on})
                    for c in range(2):
                        block = ids[j][spot + (c, owner)]
                        grad = returned[j][(other, place_on) + spot + (c,)].astype(F32)
                        totals = [totals[h] + (block == 2 * n + h).astype(F32) * grad for h in range(2)]
            for h in range(2):
                sums[j][spot + (2 * n + h,)] = totals[h].astype(BF16)
            return 0

        lax.fori_loop(0, BLOCKS // 2, two, 0)

    def across(j, hop, k):
        a1, a2, last, row, rows = PARTS[j]
        return remote(
            plane_at(sums[j], last, **{a1: k, a2: (me[a2] + hop) % SIDE}),
            landed[j].at[hop - 1, k],
            s1.at[j, hop - 1, k],
            v1.at[j, hop - 1, k],
            moved(me, a2, hop),
        )

    def bands(group):
        done(sent[group])

        def one(k, _):
            for j in range(3):
                fold(j, group, k)
                if group:
                    across(j, group, k).start()
            return 0

        lax.fori_loop(0, SIDE, one, 0)

    give(1)
    own[0].wait()
    halves.wait()
    h0[...] = h0[...] + b0[...]
    stage = weigh(0, 2, lambda j, k: h0.at[j, k], lambda j, h: b1.at[j, h])
    give(3)
    for copy in own[1:]:
        copy.wait()
    bands(1)
    done(stage)
    for j, part in enumerate(PARTS):
        h1[j] = h0[j, me[part[2]]] + b1[j, 0] + b1[j, 1] + b1[j, 2]
    stage = weigh(1, 1, lambda j, k: h1.at[j, k], lambda j, h: b2.at[j, h])
    give(2)
    bands(3)
    done(stage)
    for j, part in enumerate(PARTS):
        h2[j] = h1[j, me[part[1]]] + b2[j, 0] + b2[j, 1] + b2[j, 2]
    stage = weigh(2, 0, lambda j, k: h2.at[j, k], lambda j, h: b3.at[j, h])
    give(0)
    bands(2)
    done(stage)
    for j, part in enumerate(PARTS):
        piece(j, 3)[...] = (h2[j, me[part[0]]] + b3[j, 0] + b3[j, 1] + b3[j, 2]) * scale[0]
    stage = weigh(3, 0, lambda j, k: piece(j, 3), lambda j, h: piece(j, 3))
    bands(0)
    done(stage)
    stage = weigh(4, 1, lambda j, k: piece(j, 2), lambda j, h: piece(j, 2))
    for hop in HOPS:
        for j in range(3):
            for k in range(SIDE):
                across(j, hop, k).wait()
    done(stage)
    stage = weigh(5, 2, lambda j, k: piece(j, 1), lambda j, h: piece(j, 1))
    second = []
    for hop in HOPS + (0,):
        for j, (a1, a2, last, row, rows) in enumerate(PARTS):
            k = (me[a1] + hop) % SIDE
            mine = plane_at(sums[j], last, **{a1: k, a2: me[a2]})

            def add(n, _, j=j, k=k, hop=hop, mine=mine):
                total = mine[n].astype(F32)
                for h in range(3):
                    total = total + landed[j][h, k, n].astype(F32)
                held[j][hop, n] = total.astype(BF16)
                return 0

            lax.fori_loop(0, BLOCKS, add, 0)
            if hop:
                copy = remote(
                    held[j].at[hop], final[j].at[hop - 1], s2.at[j, hop - 1], v2.at[j, hop - 1], moved(me, a1, hop)
                )
                copy.start()
                second.append(copy)
    done(stage)
    back = remote(full.at[core], full.at[core], pair_sem.at[2], pair_sem.at[3], partner)
    back.start()
    done(second)
    for j, (a1, a2, last, row, rows) in enumerate(PARTS):

        def end(n, _, j=j, row=row, rows=rows):
            total = added[n, pl.ds(row, rows), :] + held[j][0, n].astype(F32)
            for h in range(3):
                total = total + final[j][h, n].astype(F32)
            out[n, pl.ds(row, rows), :] = total.astype(BF16)
            return 0

        lax.fori_loop(0, BLOCKS, end, 0)
    back.wait()


def return_grads(scale, ids, grads, extra, terms):
    dma = pltpu.SemaphoreType.DMA
    piece = (TERM_ROWS, WIDTH)
    return pl.pallas_call(
        return_kernel,
        out_shape=[
            jax.ShapeDtypeStruct((BLOCKS, ROWS, WIDTH), BF16),
            jax.ShapeDtypeStruct((CORES, 3, SIDE, SIDE, SIDE) + piece, F32),
        ],
        in_specs=[SMEM] * 4 + [ANY] * 3,
        out_specs=[VMEM] * 2,
        scratch_shapes=[pltpu.VMEM((CORES, SIDE, SIDE, SIDE, 2, rows, WIDTH), BF16) for *_, rows in PARTS]
        + [pltpu.VMEM((SIDE, SIDE, BLOCKS, rows, WIDTH), BF16) for *_, rows in PARTS]
        + [pltpu.VMEM((3, SIDE, BLOCKS, rows, WIDTH), BF16) for *_, rows in PARTS]
        + [pltpu.VMEM((SIDE, BLOCKS, rows, WIDTH), BF16) for *_, rows in PARTS]
        + [pltpu.VMEM((3, BLOCKS, rows, WIDTH), BF16) for *_, rows in PARTS]
        + [
            pltpu.VMEM((BLOCKS, ROWS, WIDTH), F32),
            pltpu.VMEM((3, SIDE, SIDE, SIDE) + piece, F32),
            pltpu.VMEM((3, SIDE, SIDE, SIDE) + piece, F32),
            pltpu.VMEM((3, SIDE, SIDE) + piece, F32),
            pltpu.VMEM((3, 3, SIDE, SIDE) + piece, F32),
            pltpu.VMEM((3, SIDE) + piece, F32),
            pltpu.VMEM((3, 3, SIDE) + piece, F32),
            pltpu.VMEM((3, 3) + piece, F32),
            dma((3, 7, SIDE)), dma((3, 7, SIDE)), dma((5,)),
            dma((3, 3, SIDE)), dma((3, 3, SIDE)), dma((3, 3)), dma((3, 3)),
            dma((4,)), dma((6, 3, 3)), dma((6, 3, 3)),
        ],
        compiler_params=pltpu.CompilerParams(collective_id=2, has_side_effects=True, vmem_limit_bytes=58 * MIB),
        name="return_grads",
    )(scale, *ids, grads, extra, terms)


def slot_specs(remote_steps):
    return [
        pl.BlockSpec((WIDE, ROWS, ROWS), lambda i: (jnp.minimum(i, remote_steps - 1), 0, 0)),
        pl.BlockSpec((WIDE, ROWS, ROWS), lambda i: (jnp.maximum(i - remote_steps, 0), 0, 0)),
    ]


def whole(shape):
    return pl.BlockSpec(shape, lambda i: (0,) * len(shape), pipeline_mode=pl.Buffered(1))


def degree_kernel(remote_steps, tgt, valid, remote_adj, local_adj, cot, scaled, norm, total):
    i = pl.program_id(0)

    @pl.when(i == 0)
    def _():
        total[...] = jnp.zeros_like(total)

    def add(adj):
        for l in range(WIDE):
            s = i * WIDE + l
            total[tgt[s]] += adj[l].astype(F32) * valid[s]

    @pl.when(i < remote_steps)
    def _():
        add(remote_adj)

    @pl.when(i >= remote_steps)
    def _():
        add(local_adj)

    @pl.when(i == pl.num_programs(0) - 1)
    def _():
        for t in range(BLOCKS):
            row_norm = lax.rsqrt(1.0 + jnp.sum(total[t], axis=1, keepdims=True))
            scaled[t] = (cot[t].astype(F32) * row_norm).astype(BF16)
            norm[t] = jnp.broadcast_to(row_norm, (ROWS, ROWS))


def degrees(tgt, valid, remote_adj, local_adj, cot):
    remote_steps, local_steps = remote_adj.shape[0] // WIDE, local_adj.shape[0] // WIDE
    return pl.pallas_call(
        functools.partial(degree_kernel, remote_steps),
        grid=(remote_steps + local_steps,),
        out_shape=[
            jax.ShapeDtypeStruct((BLOCKS, ROWS, WIDTH), BF16),
            jax.ShapeDtypeStruct((BLOCKS, ROWS, ROWS), F32),
        ],
        in_specs=[SMEM] * 2 + slot_specs(remote_steps) + [whole((BLOCKS, ROWS, WIDTH))],
        out_specs=[whole((BLOCKS, ROWS, WIDTH)), whole((BLOCKS, ROWS, ROWS))],
        scratch_shapes=[pltpu.VMEM((BLOCKS, ROWS, ROWS), F32)],
        compiler_params=pltpu.CompilerParams(vmem_limit_bytes=32 * MIB),
        name="degrees",
    )(tgt, valid, remote_adj, local_adj, cot)


def forward_kernel(
    remote_steps, tgt, rel, valid, src, coeffs, remote_adj, local_adj, incoming, feats, weights, scaled, cot, norm,
    self_weight, bases, out, terms, mixed, outer, held, inner,
):
    i = pl.program_id(0)

    @pl.when(i == 0)
    def _():
        mixed[...] = jnp.zeros_like(mixed)
        outer[...] = jnp.zeros_like(outer)

    def visit(adj, rows_of):
        for l in range(WIDE):
            rows = jnp.dot(adj[l], rows_of(l), preferred_element_type=F32)
            held[l] = (rows * valid[i * WIDE + l]).astype(BF16)
        for l in range(WIDE):
            s = i * WIDE + l
            mixed[tgt[s]] += jnp.dot(held[l], weights[rel[s]], preferred_element_type=F32)
            outer[rel[s]] += lax.dot_general(
                held[l], scaled[tgt[s]], (((0,), (0,)), ((), ())), preferred_element_type=F32
            )

    @pl.when(i < remote_steps)
    def _():
        visit(remote_adj, lambda l: incoming[l])

    @pl.when(i >= remote_steps)
    def _():
        visit(local_adj, lambda l: feats[src[(i - remote_steps) * WIDE + l]])

    @pl.when(i == pl.num_programs(0) - 1)
    def _():
        relations = outer.shape[0]
        basis_count = bases.shape[0]
        for t in range(BLOCKS):
            own = jnp.dot(feats[t], self_weight[...], preferred_element_type=F32)
            for half in range(2):
                cols = pl.ds(half * ROWS, ROWS)
                out[t, :, cols] = (
                    norm[t] * mixed[t, :, cols] + own[:, half * ROWS : (half + 1) * ROWS]
                ).astype(BF16)
        self_grad = jnp.zeros((WIDTH, WIDTH), F32)
        for t in range(BLOCKS):
            self_grad += lax.dot_general(feats[t], cot[t], (((0,), (0,)), ((), ())), preferred_element_type=F32)
        terms[pl.ds(basis_count * WIDTH, WIDTH), :] = self_grad

        def mix(n, _):
            for half in range(2):
                totals = [jnp.zeros((32, WIDTH), F32)] * 4
                for r in range(relations):
                    piece = outer[r, pl.ds(n * 32, 32), :]
                    totals = [totals[b] + coeffs[r, half * 4 + b] * piece for b in range(4)]
                for b in range(4):
                    terms[pl.ds((half * 4 + b) * WIDTH + n * 32, 32), :] = totals[b]
            return 0

        lax.fori_loop(0, WIDTH // 32, mix, 0)
        inner[...] = jnp.zeros_like(inner)

        def products(n, _):
            rows = pl.ds(n * 16, 16)
            pieces = [bases[b, rows, :].astype(F32) for b in range(basis_count)]
            for r in range(relations):
                piece = outer[r, rows, :]
                for b in range(basis_count):
                    both = piece * pieces[b]
                    both = both[:8] + both[8:]
                    inner[r * basis_count + b] += both[:, :ROWS] + both[:, ROWS:]
            return 0

        lax.fori_loop(0, WIDTH // 16, products, 0)
        coef_rows = pl.ds((basis_count + 1) * WIDTH, relations * basis_count)
        terms[coef_rows, pl.ds(0, ROWS)] = jnp.sum(inner[...], axis=1)
        terms[coef_rows, pl.ds(ROWS, ROWS)] = jnp.zeros((relations * basis_count, ROWS), F32)
        used = (basis_count + 1) * WIDTH + relations * basis_count
        terms[pl.ds(used, TERMS - used), :] = jnp.zeros((TERMS - used, WIDTH), F32)


def forward_slots(
    tgt, rel, valid, src, coeffs, remote_adj, local_adj, incoming, feats, weights, scaled, cot, norm, self_weight, bases
):
    remote_steps, local_steps = remote_adj.shape[0] // WIDE, local_adj.shape[0] // WIDE
    relations, basis_count = coeffs.shape
    return pl.pallas_call(
        functools.partial(forward_kernel, remote_steps),
        grid=(remote_steps + local_steps,),
        out_shape=[
            jax.ShapeDtypeStruct((BLOCKS, ROWS, WIDTH), BF16),
            jax.ShapeDtypeStruct((TERMS, WIDTH), F32),
        ],
        in_specs=[SMEM] * 5
        + slot_specs(remote_steps)
        + [pl.BlockSpec((WIDE, ROWS, WIDTH), lambda i: (jnp.minimum(i, remote_steps - 1), 0, 0))]
        + [whole(a.shape) for a in (feats, weights, scaled, cot, norm, self_weight, bases)],
        out_specs=[whole((BLOCKS, ROWS, WIDTH)), whole((TERMS, WIDTH))],
        scratch_shapes=[
            pltpu.VMEM((BLOCKS, ROWS, WIDTH), F32),
            pltpu.VMEM((relations, WIDTH, WIDTH), F32),
            pltpu.VMEM((WIDE, ROWS, WIDTH), BF16),
            pltpu.VMEM((relations * basis_count, 8, ROWS), F32),
        ],
        compiler_params=pltpu.CompilerParams(vmem_limit_bytes=48 * MIB),
        name="forward_slots",
    )(tgt, rel, valid, src, coeffs, remote_adj, local_adj, incoming, feats, weights, scaled, cot, norm, self_weight, bases)


def local(
    node_feats, send_block, recv_block, recv_rel, recv_count, recv_adj, local_src, local_tgt, local_rel, local_adj,
    bases, coeffs, self_weight, cotangent,
):
    peers = lax.axis_size(("src", "tgt"))
    slot_cap = send_block.shape[2]
    remote_slots = peers * slot_cap
    relations, basis_count = coeffs.shape
    feats = node_feats.reshape(BLOCKS, ROWS, WIDTH)
    cot = cotangent.reshape(BLOCKS, ROWS, WIDTH)
    remote_adj = recv_adj.reshape(remote_slots, ROWS, ROWS)
    own_adj = local_adj[0]
    src = local_src[0]
    tgt = jnp.concatenate([recv_block.reshape(remote_slots), local_tgt[0]])
    rel = jnp.concatenate([recv_rel.reshape(remote_slots), local_rel[0]])
    remote_valid = (jnp.arange(slot_cap, dtype=jnp.int32)[None, :] < recv_count[0][:, None]).astype(F32)
    valid = jnp.concatenate([remote_valid.reshape(remote_slots), jnp.ones((src.shape[0],), F32)])
    wide_coeffs = coeffs.astype(F32)
    scaled, norm = degrees(tgt, valid, remote_adj, own_adj, cot)
    *gathered, weights, extra, grads = gather_plane(
        wide_coeffs, tgt, rel, valid, src, feats, send_block[0].T, bases, scaled, cot, self_weight, remote_adj, own_adj
    )
    gathered, ids = gathered[:3], gathered[3:]
    incoming = exchange_picks(gathered, ids).reshape(remote_slots, ROWS, WIDTH)
    features_out, terms = forward_slots(
        tgt, rel, valid, src, wide_coeffs, remote_adj, own_adj, incoming, feats, weights, scaled, cot, norm,
        self_weight, bases,
    )
    scale = jnp.full((1,), 1.0 / math.sqrt(node_feats.shape[0] * peers), F32)
    grad_features, totals = return_grads(
        scale,
        ids,
        grads.reshape(SIDE, CORES, SIDE, SIDE, slot_cap, ROWS, WIDTH),
        extra,
        terms.reshape(CORES, 3, SIDE, SIDE, SIDE, TERM_ROWS, WIDTH),
    )
    totals = totals.reshape(TERMS, WIDTH)
    basis_rows = basis_count * WIDTH
    return (
        features_out.reshape(node_feats.shape),
        grad_features.reshape(node_feats.shape),
        totals[:basis_rows].reshape(basis_count, WIDTH, WIDTH),
        jnp.sum(totals[basis_rows + WIDTH : basis_rows + WIDTH + relations * basis_count], axis=1).reshape(relations, basis_count),
        totals[basis_rows : basis_rows + WIDTH],
    )


def solution(mesh):
    both = ("src", "tgt")
    in_specs = (
        P(both, None),
        P(both, None, None),
        P(both, None, None),
        P(both, None, None),
        P(both, None),
        P(both, None, None, None, None),
        P(both, None),
        P(both, None),
        P(both, None),
        P(both, None, None, None),
        P(),
        P(),
        P(),
        P(both, None),
    )
    out_specs = (P(both, None), P(both, None), P(), P(), P())
    return jax.shard_map(local, mesh=mesh, in_specs=in_specs, out_specs=out_specs, check_vma=False)
```

time: 463 us -> 354 us (0.76)
  Pallas kernels: 414 us -> 327 us
  between operations: 14.3 us -> 0.9 us
  local copies, waits for them, and re-layouts: 29.4 us -> 21.5 us
    pallas_call x1, Pallas kernels: 86.1 us -> 42.6 us  [forward_slots(): pl.pallas_call(functools.partial(forward_kernel, remote_steps), grid=(rem...]
    pallas_call x6 -> x2, Pallas kernels: 246 us -> 203 us  [the longest x1 147 us: return_grads(): pl.pallas_call(return_kernel, out_shape=[jax.ShapeDtypeStruct((BLOCKS, RO...]
    unnamed x49 -> x51, local copies, waits for them, and re-layouts: 26.5 us -> 16.3 us
  transfers between devices with their start and end apart: 1 -> 0, of which waited for: 0 -> 0; matrix products, arithmetic and copies ran while one was open for 0% -> 0% of each run, Pallas kernels for 39% -> 0%
where the time goes in v2:
time: 354 us; the launch traced here: 353 us
  Pallas kernels  327 us (92%)
  local copies, waits for them, and re-layouts  21.5 us (6%)
  other arithmetic  3.73 us (1%)
    pallas_call x1, Pallas kernels, return_grads(): pl.pallas_call(return_kernel, out_shape=[jax.ShapeDtypeStruct((BLOCKS, RO...  147 us
    pallas_call x1, Pallas kernels, exchange_picks(): pl.pallas_call(exchange_kernel, out_shape=jax.ShapeDtypeStruct((SIDE, COR...  77.2 us
    pallas_call x1, Pallas kernels, gather_plane(): pl.pallas_call(gather_kernel, out_shape=shapes, in_specs=[SMEM] * 5 + [AN...  56 us
    pallas_call x1, Pallas kernels, forward_slots(): pl.pallas_call(functools.partial(forward_kernel, remote_steps), grid=(rem...  42.6 us
    unnamed x51, local copies, waits for them, and re-layouts  16.3 us

profile of v2, /device:TPU:1, one launch (start us, length us, event | category | flops | bytes accessed | tf_op | source)
XLA Modules:
  0.0 353.3 jit_solution(2619162407991586467)
XLA Ops:
  0.6 0.8 copy.22
  1.4 0.6 convert_element_type.9.coeffs
  2.0 0.7 iota_compare_fusion
  2.8 0.1 convert_element_type.8
  2.9 0.8 copy.20
  3.7 0.1 reshape.56
  3.9 0.8 copy.21
  4.6 0.1 reshape.57
  4.8 1.3 pad_add_fusion
  6.1 3.4 copy-done
  9.4 1.6 copy-done.1
  11.0 1.0 copy-done.3
  12.1 4.1 %degrees.1 = (bf16[8,128,256]{2,1,0:T(8,128)(2,1)S(1)}, f32[8,128,128]{2,1,0:T(8,128)S(1)}) custom-call(s32[320]{0:T(512)S(1)} %get-tuple-element.40.tgt, f32[320]{0:T(512)S(1)} %pad_convert_fusion.valid, bf16[256,128,128]{2,1,0:T(8,128)(2,1)S(1)} %bitcast.20, bf16[64,128,128]{2,1,0:T(8,128)(2,1)S(1)} %bitcast.22, bf16[8,128,256]{2,1,0:T(8,128)(2,1)S(1)} %bitcast.25), custom_call_target="tpu_custom_call" | custom-call | tf_op jit(solution)/shard_map/degrees/pallas_call | solution.py:541
  16.2 0.0 copy-start.8
  16.2 0.8 copy-done.8
  17.0 56.0 %gather_plane.1 = (bf16[4,4,8,48,256]{4,3,2,1,0:T(8,128)(2,1)}, bf16[4,4,8,48,256]{4,3,2,1,0:T(8,128)(2,1)}, bf16[4,4,8,32,256]{4,3,2,1,0:T(8,128)(2,1)}, s32[4,...) custom-call(f32[30,8]{1,0:T(8,128)} %convert_element_type.9.coeffs, ...), custom_call_target="tpu_custom_call" | custom-call | tf_op jit(solution)/shard_map/gather_plane/pallas_call | solution.py:216
  73.0 1.9 copy-done.6
  74.9 1.6 copy-done.10
  76.5 0.7 copy-done.13
  77.2 0.7 copy-done.14
  77.9 0.7 copy-done.15
  78.7 0.0 copy-start.12
  78.7 0.0 copy-start.17
  78.7 77.2 %exchange_picks.1 = bf16[4,2,4,4,2,128,256]{6,5,4,3,2,1,0:T(8,128)(2,1)} custom-call(bf16[4,4,8,48,256]{4,3,2,1,0:T(8,128)(2,1)S(1)} %copy-done.6, bf16[4,4,8,48,256]{4,3,2,1,0:T(8,128)(2,1)} %get-tuple-element.22.g1, bf16[4,4,8,32,256]{4,3,2,1,0:T(8,128)(2,1)S(1)} %copy-done.10, s32[4,4,2,128]{3,2,1,0:T(2,128)S(1)} %copy-done.13, ...), custom_call_target="tpu_custom_call" | custom-call | tf_op jit(solution)/shard_map/exchange_picks/pallas_call | solution.py:276
  156.0 42.6 %forward_slots.1 = (bf16[8,128,256]{2,1,0:T(8,128)(2,1)}, f32[3072,256]{1,0:T(8,128)}) custom-call(s32[320]{0:T(512)S(1)} %copy-done.19, s32[320]{0:T(512)S(1)} %copy-done.20, f32[320]{0:T(512)S(1)} %copy-done.17, s32[64]{0:T(128)S(1)} %bitcast.30, f32[30,8]{1,0:T(8,128)S(1)} %copy-done.12, bf16[256,128,128]{2,1,0:T(8,128)(2,1)} %bitcast.19, ...), custom_call_target="tpu_custom_call" | custom-call | tf_op jit(solution)/shard_map/forward_slots/pallas_call | solution.py:639
  198.6 147.3 %return_grads.1 = (bf16[8,128,256]{2,1,0:T(8,128)(2,1)}, f32[2,3,4,4,4,8,256]{6,5,4,3,2,1,0:T(8,128)}) custom-call(f32[1]{0:T(128)} %constant.2.clone.1.scale, s32[4,4,2,128]{3,2,1,0:T(2,128)} %get-tuple-element.24.i0, s32[4,4,2,128]{3,2,1,0:T(2,128)} %get-tuple-element.25.i1, s32[4,4,2,128]{3,2,1,0:T(2,128)} %get-tuple-element.26.i2, ...), custom_call_target="tpu_custom_call" | custom-call | tf_op jit(solution)/shard_map/return_grads/pallas_call | solution.py:469
  346.0 1.1 slice_reduce_fusion
  347.1 0.1 reshape.68
  347.2 0.7 copy.23
  347.8 1.7 slice.14
  349.5 3.0 slice.12
  352.6 0.8 copy.25
  (35 shorter events, 0.1 us)
Async XLA Ops:
  2.9 13.2 %copy-start.16 = (f32[320]{0:T(512)}, f32[320]{0:T(512)S(1)}, u32[]{:S(2)}) copy-start(f32[320]{0:T(512)S(1)} %pad_convert_fusion.valid) | copy-start | bytes 3844
  6.0 10.1 %copy-start.18 = (s32[320]{0:T(512)}, s32[320]{0:T(512)S(1)}, u32[]{:S(2)}) copy-start(s32[320]{0:T(512)S(1)} %get-tuple-element.40.tgt) | copy-start | bytes 3844
  6.1 3.4 copy-start
  9.4 1.6 copy-start.1
  11.0 1.0 copy-start.3
  16.2 0.8 copy-start.8
  73.0 1.9 copy-start.6
  74.9 1.6 copy-start.10
  76.5 0.7 copy-start.13
  77.2 0.7 copy-start.14
  77.9 0.7 copy-start.15
  78.6 77.3 %copy-start.2 = (bf16[1,64,128,128]{3,2,1,0:T(8,128)(2,1)S(1)}, bf16[1,64,128,128]{3,2,1,0:T(8,128)(2,1)}, u32[]{:S(2)}) copy-start(bf16[1,64,128,128]{3,2,1,0:T(8,128)(2,1)} %param.23) | copy-start | bytes 6291460
  78.6 77.3 %copy-start.4 = (bf16[1024,256]{1,0:T(8,128)(2,1)S(1)}, bf16[1024,256]{1,0:T(8,128)(2,1)}, u32[]{:S(2)}) copy-start(bf16[1024,256]{1,0:T(8,128)(2,1)} %param.27) | copy-start | bytes 1572868
  78.6 77.3 %copy-start.5 = (bf16[8,256,256]{2,1,0:T(8,128)(2,1)S(1)}, bf16[8,256,256]{2,1,0:T(8,128)(2,1)}, u32[]{:S(2)}) copy-start(bf16[8,256,256]{2,1,0:T(8,128)(2,1)} %bases.3) | copy-start | bytes 3145732
  78.6 77.3 %copy-start.7 = (bf16[1024,256]{1,0:T(8,128)(2,1)S(1)}, bf16[1024,256]{1,0:T(8,128)(2,1)}, u32[]{:S(2)}) copy-start(bf16[1024,256]{1,0:T(8,128)(2,1)} %param.14) | copy-start | bytes 1572868
  78.7 77.3 %copy-start.9 = (bf16[8,128,256]{2,1,0:T(8,128)(2,1)S(1)}, bf16[8,128,256]{2,1,0:T(8,128)(2,1)}, u32[]{:S(2)}) copy-start(bf16[8,128,256]{2,1,0:T(8,128)(2,1)} %copy-done.8) | copy-start | bytes 1572868
  78.7 77.3 %copy-start.11 = (bf16[256,256]{1,0:T(8,128)(2,1)S(1)}, bf16[256,256]{1,0:T(8,128)(2,1)}, u32[]{:S(2)}) copy-start(bf16[256,256]{1,0:T(8,128)(2,1)} %self_weight.3) | copy-start | bytes 393220
  78.7 77.3 %copy-start.12 = (f32[30,8]{1,0:T(8,128)S(1)}, f32[30,8]{1,0:T(8,128)}, u32[]{:S(2)}) copy-start(f32[30,8]{1,0:T(8,128)} %convert_element_type.9.coeffs) | copy-start | bytes 2884
  78.7 77.3 %copy-start.17 = (f32[320]{0:T(512)S(1)}, f32[320]{0:T(512)}, u32[]{:S(2)}) copy-start(f32[320]{0:T(512)} %copy-done.16) | copy-start | bytes 3844
  78.7 77.3 %copy-start.19 = (s32[320]{0:T(512)S(1)}, s32[320]{0:T(512)}, u32[]{:S(2)}) copy-start(s32[320]{0:T(512)} %copy-done.18) | copy-start | bytes 3844
  78.7 77.3 %copy-start.20 = (s32[320]{0:T(512)S(1)}, s32[320]{0:T(512)}, u32[]{:S(2)}) copy-start(s32[320]{0:T(512)} %get-tuple-element.41.rel) | copy-start | bytes 3844
  78.7 77.3 %copy-start.21 = (s32[1,64]{1,0:T(1,128)S(1)}, s32[1,64]{1,0:T(1,128)}, u32[]{:S(2)}) copy-start(s32[1,64]{1,0:T(1,128)} %param.20) | copy-start | bytes 772
  345.9 6.6 %copy-start.22 = (bf16[8,128,256]{2,1,0:T(8,128)(2,1)S(1)}, bf16[8,128,256]{2,1,0:T(8,128)(2,1)}, u32[]{:S(2)}) copy-start(bf16[8,128,256]{2,1,0:T(8,128)(2,1)} %get-tuple-element.33) | copy-start | bytes 1572868

commit v3 on v2

v3 whole, which is shorter than its diff:
```python
import functools
import math

import jax
import jax.numpy as jnp
from jax import lax
from jax.experimental import pallas as pl
from jax.experimental.pallas import tpu as pltpu
from jax.sharding import PartitionSpec as P

MESH = pl.DeviceIdType.MESH
MIB = 1 << 20
F32 = jnp.float32
BF16 = jnp.bfloat16
SIDE = 4
CORES = 2
BLOCKS = 8
ROWS = 128
WIDTH = 256
STEP = 8
WIDE = 32
PIECES = 4
CHUNKS = 8
TERM_ROWS = 8
PARTS = (("x", "y", "z", 0, 48), ("y", "z", "x", 48, 48), ("z", "x", "y", 96, 32))
AXES = ("y", "z", "x")
HOPS = (1, 3, 2)
ANY = pl.BlockSpec(memory_space=pl.ANY)
VMEM = pl.BlockSpec(memory_space=pltpu.VMEM)
SMEM = pl.BlockSpec(memory_space=pltpu.SMEM)


def place():
    src, tgt = lax.axis_index("src"), lax.axis_index("tgt")
    return {"y": src // CORES, "c": src % CORES, "z": tgt // SIDE, "x": tgt % SIDE}


def device(at):
    return (at["y"] * CORES + at["c"], at["z"] * SIDE + at["x"])


def band(at):
    return (at["y"] * CORES + at["c"]) * SIDE * SIDE + at["z"] * SIDE + at["x"]


def moved(me, axis, hop):
    return {**me, axis: (me[axis] + hop) % SIDE}


def line_peers(me, axis):
    peers = []
    for hop in HOPS:
        for flip in (0, 1):
            peers.append((hop, flip, {**moved(me, axis, hop), "c": (me["c"] + flip) % CORES}))
    peers.append((0, 1, {**me, "c": (me["c"] + 1) % CORES}))
    return peers


def greet(peers):
    barrier = pltpu.get_barrier_semaphore()
    for peer in peers:
        pl.semaphore_signal(barrier, inc=1, device_id=device(peer), device_id_type=MESH)
    pl.semaphore_wait(barrier, len(peers))


def plane_dims(last):
    return tuple(a for a in AXES if a != last)


def plane_at(ref, last, **where):
    return ref.at[tuple(where.get(a, slice(None)) for a in plane_dims(last))]


def band_at(ref, core, row, rows, **where):
    where = {"y": slice(None), "z": slice(None), "x": slice(None), **where}
    return ref.at[where["y"], core, where["z"], where["x"], :, pl.ds(row, rows), :]


def remote(src, dst, send, recv, peer):
    return pltpu.make_async_remote_copy(
        src_ref=src, dst_ref=dst, send_sem=send, recv_sem=recv, device_id=device(peer), device_id_type=MESH
    )


def spread_kernel(
    coeffs, recv_tgt, recv_rel, recv_count, local_tgt, local_rel, src, feats, picks, bases, scaled, cot, self_weight, remote_adj, local_adj,
    incoming, i0, i1, i2, weights, extra, grads, self_out, self_grad,
    feats_here, *refs,
):
    gathered, refs = (refs[0:4], refs[4:8], refs[8:12]), refs[12:]
    (
        t0, t1, t2, b0, b1, b2, adj, own_adj, cots, staged, part,
        own_sem, adj_sem, out_sem, is1, ir1, is2, ir2, table_sem, gs1, gr1, gs2, gr2, send, recv, self_sem,
    ) = refs
    me = place()
    ids, tables, packed = (i0, i1, i2), (t0, t1, t2), (b0, b1, b2)
    relations, remote_slots, local_slots = cots.shape[0], adj.shape[0], own_adj.shape[0]
    chunk = remote_slots // CHUNKS
    partner = {**me, "c": (me["c"] + 1) % CORES}
    adj_copies = [
        pltpu.make_async_copy(remote_adj, adj, adj_sem.at[0]),
        pltpu.make_async_copy(local_adj, own_adj, adj_sem.at[1]),
        pltpu.make_async_copy(feats, feats_here, adj_sem.at[2]),
    ]
    own = []
    for j, (a1, a2, last, row, rows) in enumerate(PARTS):
        here = {a1: me[a1], a2: me[a2]}
        own.append(
            pltpu.make_async_copy(feats.at[:, pl.ds(row, rows), :], gathered[j][0].at[me[a1]], own_sem.at[j, 0])
        )
        own.append(pltpu.make_async_copy(picks, plane_at(ids[j], last, **here), own_sem.at[j, 1]))
    for copy in own + adj_copies:
        copy.start()
    greet([p for axis in AXES for hop, flip, p in line_peers(me, axis) if hop] + [partner])

    def begin(copies):
        for copy in copies:
            copy.start()
        return copies

    def done(copies):
        for copy in copies:
            copy.wait()

    def column(j, e, far=0):
        return gathered[j][far].at[(me[PARTS[j][0]] + e) % SIDE]

    ids_first = begin(
        [
            remote(
                picks, plane_at(ids[j], last, **{a1: me[a1], a2: me[a2]}), is1.at[j, h - 1], ir1.at[j, h - 1],
                moved(me, a1, h),
            )
            for h in HOPS
            for j, (a1, a2, last, row, rows) in enumerate(PARTS)
        ]
    )
    first = {}
    for way, hop in enumerate((1, 3)):
        for j, (a1, a2, last, row, rows) in enumerate(PARTS):
            first[j, way, 0] = remote(
                feats.at[:, pl.ds(row, rows), :], column(j, 0), gs1.at[j, way, 0], gr1.at[j, way, 0],
                moved(me, a1, hop),
            )
            first[j, way, 0].start()
    done(ids_first)
    done([own[1], own[3], own[5]])
    ids_rest = begin(
        [
            remote(
                plane_at(ids[j], last, **{a2: me[a2]}), plane_at(ids[j], last, **{a2: me[a2]}),
                is2.at[j, h - 1], ir2.at[j, h - 1], moved(me, a2, h),
            )
            for h in HOPS
            for j, (a1, a2, last, row, rows) in enumerate(PARTS)
        ]
    )
    second = {}

    def onward(e):
        for way, hop in enumerate((1, 3)):
            for j, (a1, a2, last, row, rows) in enumerate(PARTS):
                from_ = column(j, e) if e else feats.at[:, pl.ds(row, rows), :]
                second[j, e, way, 0] = remote(
                    from_, column(j, e, (3, 1)[way]), gs2.at[j, e, way, 0], gr2.at[j, e, way, 0], moved(me, a2, hop)
                )
                second[j, e, way, 0].start()

    onward(0)

    def mix(r, _):
        for n in range(8):
            rows = pl.ds(n * 32, 32)
            total = coeffs[r, 0] * bases[0, rows, :].astype(F32)
            for b in range(1, 8):
                total = total + coeffs[r, b] * bases[b, rows, :].astype(F32)
            weights[r, rows, :] = total.astype(BF16)
        for t in range(BLOCKS):
            cots[r, t] = lax.dot_general(
                scaled[t], weights[r], (((1,), (1,)), ((), ())), preferred_element_type=F32
            ).astype(BF16)
        return 0

    def relay_first(way):
        hop = (1, 3)[way]
        e = (3, 1)[way]
        for j, part_of in enumerate(PARTS):
            first[j, way, 0].wait_recv()
            half = column(j, e).at[pl.ds(way * 4, 4)]
            first[j, way, 1] = remote(half, half, gs1.at[j, way, 1], gr1.at[j, way, 1], moved(me, part_of[0], hop))
            first[j, way, 1].start()

    def relay_second(e):
        for way, hop in enumerate((1, 3)):
            for j, part_of in enumerate(PARTS):
                second[j, e, way, 0].wait_recv()
                half = pl.ds(way * 4, 4)
                second[j, e, way, 1] = remote(
                    column(j, e, (3, 1)[way]).at[half], column(j, e, 2).at[half], gs2.at[j, e, way, 1], gr2.at[j, e, way, 1], moved(me, part_of[1], hop)
                )
                second[j, e, way, 1].start()

    lines = {}

    def exchange(group, slot):
        lines[group] = []
        for n in range(8):
            for j, (a1, a2, last, row, rows) in enumerate(PARTS):
                peer = me if n == 7 else line_peers(me, last)[n][2]
                owner = band(peer)
                far = (me[a2] + group) % SIDE

                def one(k, _, j=j, n=n, a1=a1, a2=a2, last=last, owner=owner, far=far):
                    where = {a1: k, a2: far}
                    spot = tuple(where[a] for a in plane_dims(last))
                    for c in range(2):
                        packed[j][slot, n, k, c] = gathered[j][group][k, tables[j][spot + (c, owner)]]
                    return 0

                lax.fori_loop(0, SIDE, one, 0)
                target = band_at(incoming, me["c"], row, rows, **{last: me[last], a2: far})
                if n == 7:
                    copy = pltpu.make_async_copy(packed[j].at[slot, n], target, self_sem.at[j, group])
                else:
                    copy = remote(packed[j].at[slot, n], target, send.at[j, n, group], recv.at[j, n, group], peer)
                copy.start()
                lines[group].append(copy)

    def free(group):
        for copy in lines[group][:21]:
            copy.wait_send()
        for copy in lines[group][21:]:
            copy.wait()

    def slot_chunk(k):
        return pltpu.make_async_copy(staged.at[k % 2], grads.at[pl.ds(k * chunk, chunk)], out_sem.at[k])

    def slot_grads(low, high):
        for k in range(low, high):
            if k >= 2:
                slot_chunk(k - 2).wait()

            def group(g, _, k=k):
                for l in range(STEP):
                    peer, c = (k * chunk + g * STEP) // 2 + l // 2, l % 2
                    grad = lax.dot_general(
                        adj[2 * peer + c],
                        cots[recv_rel[c, peer], recv_tgt[c, peer]],
                        (((0,), (0,)), ((), ())),
                        preferred_element_type=F32,
                    )
                    valid = (c < recv_count[0, peer]).astype(F32)
                    staged[k % 2, g * STEP + l] = (grad * valid).astype(BF16)
                return 0

            lax.fori_loop(0, chunk // STEP, group, 0)
            slot_chunk(k).start()

    lax.fori_loop(0, 6, mix, 0)
    relay_first(0)
    relay_first(1)
    onward(3)
    onward(1)
    done(ids_rest)
    loads = begin([pltpu.make_async_copy(ids[j], tables[j], table_sem.at[j]) for j in range(3)])
    lax.fori_loop(6, 14, mix, 0)
    for j in range(3):
        for way in range(2):
            first[j, way, 1].wait_recv()
    onward(2)
    done(loads)
    done([own[0], own[2], own[4]])
    exchange(0, 0)
    relay_second(0)
    lax.fori_loop(14, 22, mix, 0)
    relay_second(3)
    relay_second(1)
    lax.fori_loop(22, relations, mix, 0)
    relay_second(2)
    exchange(1, 1)
    done(adj_copies)
    slot_grads(0, 2)
    free(0)
    exchange(3, 0)
    slot_grads(2, 4)
    for e in range(SIDE):
        for j in range(3):
            for way in range(2):
                second[j, e, way, 1].wait_recv()
    free(1)
    exchange(2, 1)
    slot_grads(4, CHUNKS)
    for t in range(BLOCKS):
        extra[t] = lax.dot_general(cot[t], self_weight[...], (((1,), (1,)), ((), ())), preferred_element_type=F32)

    def local_group(g, _):
        for l in range(STEP):
            s = g * STEP + l
            part[l] = lax.dot_general(
                own_adj[s], cots[local_rel[0, s], local_tgt[0, s]], (((0,), (0,)), ((), ())),
                preferred_element_type=F32,
            ).astype(BF16)
        for k in range(BLOCKS):
            hits = [(src[0, g * STEP + l] == k).astype(F32) for l in range(STEP)]
            for n in range(4):
                rows = pl.ds(n * 32, 32)
                total = extra[k, rows, :]
                for l in range(STEP):
                    total = total + hits[l] * part[l, rows, :].astype(F32)
                extra[k, rows, :] = total
        return 0

    lax.fori_loop(0, local_slots // STEP, local_group, 0)
    total = jnp.zeros((WIDTH, WIDTH), F32)
    for t in range(BLOCKS):
        self_out[t] = jnp.dot(feats_here[t], self_weight[...], preferred_element_type=F32)
        total += lax.dot_general(feats_here[t], cot[t], (((0,), (0,)), ((), ())), preferred_element_type=F32)
    self_grad[...] = total
    slot_chunk(CHUNKS - 2).wait()
    slot_chunk(CHUNKS - 1).wait()
    for copy in list(first.values()) + list(second.values()):
        copy.wait_send()
    free(3)
    free(2)
    for group in range(SIDE):
        for copy in lines[group][:21]:
            copy.wait_recv()


def spread_features(coeffs, slots, feats, picks, bases, scaled, cot, self_weight, remote_adj, local_adj):
    relations, remote_slots = coeffs.shape[0], remote_adj.shape[0]
    dma = pltpu.SemaphoreType.DMA
    return pl.pallas_call(
        spread_kernel,
        out_shape=[jax.ShapeDtypeStruct((SIDE, CORES, SIDE, SIDE, 2, ROWS, WIDTH), BF16)]
        + [jax.ShapeDtypeStruct((SIDE, SIDE) + picks.shape, jnp.int32)] * 3
        + [
            jax.ShapeDtypeStruct((relations, WIDTH, WIDTH), BF16),
            jax.ShapeDtypeStruct((BLOCKS, ROWS, WIDTH), F32),
            jax.ShapeDtypeStruct((remote_slots, ROWS, WIDTH), BF16),
            jax.ShapeDtypeStruct((BLOCKS, ROWS, WIDTH), F32),
            jax.ShapeDtypeStruct((WIDTH, WIDTH), F32),
        ],
        in_specs=[SMEM] * 7 + [ANY] * 2 + [VMEM] * 4 + [ANY] * 2,
        out_specs=[ANY] * 4 + [VMEM] * 2 + [ANY] + [VMEM] * 2,
        scratch_shapes=[pltpu.VMEM((BLOCKS, ROWS, WIDTH), BF16)]
        + [pltpu.VMEM((SIDE, BLOCKS, rows, WIDTH), BF16) for *_, rows in PARTS for _ in range(SIDE)]
        + [pltpu.SMEM((SIDE, SIDE) + picks.shape, jnp.int32)] * 3
        + [pltpu.VMEM((2, 8, SIDE, 2, rows, WIDTH), BF16) for *_, rows in PARTS]
        + [
            pltpu.VMEM(remote_adj.shape, BF16),
            pltpu.VMEM(local_adj.shape, BF16),
            pltpu.VMEM((relations, BLOCKS, ROWS, WIDTH), BF16),
            pltpu.VMEM((2, remote_slots // CHUNKS, ROWS, WIDTH), BF16),
            pltpu.VMEM((STEP, ROWS, WIDTH), BF16),
            dma((3, 2)), dma((3,)), dma((CHUNKS,)),
            dma((3, 3)), dma((3, 3)), dma((3, 3)), dma((3, 3)), dma((3,)),
            dma((3, 2, 2)), dma((3, 2, 2)), dma((3, SIDE, 2, 2)), dma((3, SIDE, 2, 2)),
            dma((3, 7, SIDE)), dma((3, 7, SIDE)), dma((3, SIDE)),
        ],
        compiler_params=pltpu.CompilerParams(collective_id=0, has_side_effects=True, vmem_limit_bytes=58 * MIB),
        name="spread_features",
    )(coeffs, *slots, feats, picks, bases, scaled, cot, self_weight, remote_adj, local_adj)


def return_kernel(
    coeffs, i0, i1, i2, grads, extra, outer_in, bases_in, self_grad, out, full, rest,
    r0, r1, r2, p0, p1, p2, l0, l1, l2, e0, e1, e2, q0, q1, q2, f0, f1, f2, added, outer, bases, inner, terms,
    wire, b0, b1, h1, b2, h2, b3, total,
    send, recv, own_sem, es, ev, ls, lv, s2, v2, pair_sem, ws, wr,
):
    me = place()
    ids, returned, sums, landed = (i0, i1, i2), (r0, r1, r2), (p0, p1, p2), (l0, l1, l2)
    early, held, final = (e0, e1, e2), (q0, q1, q2), (f0, f1, f2)
    core, partner = me["c"], {**me, "c": (me["c"] + 1) % CORES}
    relations, basis_count = coeffs.shape
    own = [
        pltpu.make_async_copy(outer_in, outer, own_sem.at[3]),
        pltpu.make_async_copy(bases_in, bases, own_sem.at[4]),
        pltpu.make_async_copy(self_grad, terms.at[2, 0, pl.ds(0, 2)], own_sem.at[5]),
        pltpu.make_async_copy(extra, added, own_sem.at[6]),
    ]
    for j, (a1, a2, last, row, rows) in enumerate(PARTS):
        own.append(
            pltpu.make_async_copy(
                band_at(grads, core, row, rows, **{last: me[last]}), returned[j].at[core, me[last]], own_sem.at[j]
            )
        )
    for copy in own:
        copy.start()
    greet([p for axis in AXES for hop, flip, p in line_peers(me, axis) if hop] + [partner])
    sent = [[], [], [], []]

    def give(group):
        for n in range(7):
            for j, (a1, a2, last, row, rows) in enumerate(PARTS):
                hop, flip, peer = line_peers(me, last)[n]
                far = (me[a2] + group) % SIDE
                copy = remote(
                    band_at(grads, peer["c"], row, rows, **{last: peer[last], a2: far}),
                    plane_at(returned[j].at[core, me[last]], last, **{a2: far}),
                    send.at[j, n, group],
                    recv.at[j, n, group],
                    peer,
                )
                copy.start()
                sent[group].append(copy)

    def weigh(stage, level, src, dst):
        copies = []
        for hop in HOPS:
            for j, part in enumerate(PARTS):
                axis = part[level]
                copy = remote(
                    src(j, (me[axis] + hop) % SIDE),
                    dst(j, hop - 1),
                    ws.at[stage, j, hop - 1],
                    wr.at[stage, j, hop - 1],
                    moved(me, axis, hop),
                )
                copy.start()
                copies.append(copy)
        return copies

    def done(copies):
        for copy in copies:
            copy.wait()

    def weight_terms():
        terms[2, 0, 2:4] = jnp.zeros((2, SIDE, SIDE, TERM_ROWS, WIDTH), F32)
        terms[2, 1] = jnp.zeros((SIDE, SIDE, SIDE, TERM_ROWS, WIDTH), F32)
        done(own[:3])

        def mix(n, _):
            for half in range(2):
                totals = [jnp.zeros((32, WIDTH), F32)] * 4
                for r in range(relations):
                    slab = outer[r, pl.ds(n * 32, 32), :]
                    totals = [totals[b] + coeffs[r, half * 4 + b] * slab for b in range(4)]
                for b in range(4):
                    terms[half, b // 2, (b % 2) * 2 + n // 4, n % 4] = totals[b].reshape(4, TERM_ROWS, WIDTH)
            return 0

        lax.fori_loop(0, WIDTH // 32, mix, 0)
        inner[...] = jnp.zeros_like(inner)

        def products(n, _):
            rows = pl.ds(n * 16, 16)
            slabs = [bases[b, rows, :].astype(F32) for b in range(basis_count)]
            for r in range(relations):
                slab = outer[r, rows, :]
                for b in range(basis_count):
                    both = slab * slabs[b]
                    both = both[:8] + both[8:]
                    inner[r * basis_count + b] += both[:, :ROWS] + both[:, ROWS:]
            return 0

        lax.fori_loop(0, WIDTH // 16, products, 0)
        for r in range(relations):
            terms[2, 0, 2 + r // 16, (r // 4) % 4, r % 4, :, pl.ds(0, ROWS)] = jnp.sum(
                inner[pl.ds(r * basis_count, basis_count)], axis=1
            )

    def piece(j, depth):
        spot = tuple(me[PARTS[j][level]] for level in (2, 1, 0)[:depth])
        return total.at[(j, core) + spot]

    def add(*parts):
        return sum(part.astype(F32) for part in parts[1:]) + parts[0].astype(F32)

    def spot_of(j, group, k):
        a1, a2, last, row, rows = PARTS[j]
        where = {a1: k, a2: (me[a2] + group) % SIDE}
        return tuple(where[a] for a in plane_dims(last))

    def fold(j, group, k, low, high, way=None):
        a1, a2, last, row, rows = PARTS[j]
        spot = spot_of(j, group, k)

        def two(n, _):
            if way is None:
                totals = [jnp.zeros((rows, WIDTH), F32)] * 2
            else:
                totals = [early[j][way, k, 2 * n + h - low].astype(F32) for h in range(2)]
            for other in range(CORES):
                for place_on in range(SIDE):
                    owner = band({**me, "c": other, last: place_on})
                    for c in range(2):
                        block = ids[j][spot + (c, owner)]
                        grad = returned[j][(other, place_on) + spot + (c,)].astype(F32)
                        totals = [totals[h] + (block == 2 * n + h).astype(F32) * grad for h in range(2)]
            for h in range(2):
                sums[j][spot + (2 * n + h,)] = totals[h].astype(BF16)
            return 0

        lax.fori_loop(low // 2, high // 2, two, 0)

    def half_on(j, way, k):
        return remote(
            sums[j].at[spot_of(j, 2, k) + (pl.ds(way * 4, 4),)], early[j].at[way, k], es.at[j, way, k],
            ev.at[j, way, k], moved(me, PARTS[j][1], (1, 3)[way]),
        )

    def across(j, way, late, k):
        low = 4 * way if late else 4 - 4 * way
        return remote(
            sums[j].at[spot_of(j, (1, 3)[way], k) + (pl.ds(low, 4),)], landed[j].at[way, k, pl.ds(low, 4)],
            ls.at[j, way, late, k], lv.at[j, way, late, k], moved(me, PARTS[j][1], (1, 3)[way]),
        )

    def each_band(work):
        def one(k, _):
            for j in range(3):
                work(j, k)
            return 0

        lax.fori_loop(0, SIDE, one, 0)

    def far_bands(j, k):
        fold(j, 2, k, 0, BLOCKS)
        half_on(j, 0, k).start()
        half_on(j, 1, k).start()

    def near_bands(way, late):
        def work(j, k):
            low = 4 * way if late else 4 - 4 * way
            if late:
                half_on(j, way, k).wait()
            fold(j, (1, 3)[way], k, low, low + 4, way if late else None)
            across(j, way, late, k).start()

        return work

    give(2)
    give(1)
    weight_terms()
    for j in range(3):
        for c in range(CORES):
            for k in range(SIDE):
                slab = terms[j, c, k]
                wire[j, c, k] = jnp.concatenate([slab[..., :ROWS], slab[..., ROWS:]], axis=2).astype(BF16)
    halves = remote(wire.at[:, partner["c"]], b0, pair_sem.at[0], pair_sem.at[1], partner)
    halves.start()
    give(3)
    done(own[3:])
    done(sent[2])
    each_band(far_bands)
    halves.wait()
    b0[...] = add(wire[:, core], b0[...]).astype(BF16)
    stage = weigh(0, 2, lambda j, k: b0.at[j, k], lambda j, h: b1.at[j, h])
    give(0)
    done(sent[1])
    each_band(near_bands(0, 0))
    done(stage)
    for j, part in enumerate(PARTS):
        h1[j] = add(b0[j, me[part[2]]], b1[j, 0], b1[j, 1], b1[j, 2]).astype(BF16)
    stage = weigh(1, 1, lambda j, k: h1.at[j, k], lambda j, h: b2.at[j, h])
    done(sent[3])
    each_band(near_bands(1, 0))
    done(stage)
    for j, part in enumerate(PARTS):
        h2[j] = add(h1[j, me[part[1]]], b2[j, 0], b2[j, 1], b2[j, 2]).astype(BF16)
    stage = weigh(2, 0, lambda j, k: h2.at[j, k], lambda j, h: b3.at[j, h])
    each_band(near_bands(0, 1))
    each_band(near_bands(1, 1))
    done(stage)
    for j, part in enumerate(PARTS):
        piece(j, 3)[...] = add(h2[j, me[part[0]]], b3[j, 0], b3[j, 1], b3[j, 2]).astype(BF16)
    stage = weigh(3, 0, lambda j, k: piece(j, 3), lambda j, h: piece(j, 3))
    done(sent[0])
    each_band(lambda j, k: fold(j, 0, k, 0, BLOCKS))
    done(stage)
    stage = weigh(4, 1, lambda j, k: piece(j, 2), lambda j, h: piece(j, 2))
    for j in range(3):
        for way in range(2):
            for late in range(2):
                for k in range(SIDE):
                    across(j, way, late, k).wait()
    second = []
    for hop in HOPS + (0,):
        for j, (a1, a2, last, row, rows) in enumerate(PARTS):
            k = (me[a1] + hop) % SIDE
            mine = sums[j].at[spot_of(j, 0, k)]

            def join(n, _, j=j, k=k, hop=hop, mine=mine):
                both = mine[n].astype(F32) + landed[j][0, k, n].astype(F32) + landed[j][1, k, n].astype(F32)
                held[j][hop, n] = both.astype(BF16)
                return 0

            lax.fori_loop(0, BLOCKS, join, 0)
            if hop:
                copy = remote(
                    held[j].at[hop], final[j].at[hop - 1], s2.at[j, hop - 1], v2.at[j, hop - 1], moved(me, a1, hop)
                )
                copy.start()
                second.append(copy)
    done(stage)
    stage = weigh(5, 2, lambda j, k: piece(j, 1), lambda j, h: piece(j, 1))
    done(second)
    done(stage)
    back = remote(total.at[:, core], total.at[:, core], pair_sem.at[2], pair_sem.at[3], partner)
    back.start()
    for j, (a1, a2, last, row, rows) in enumerate(PARTS):

        def end(n, _, j=j, row=row, rows=rows):
            both = added[n, pl.ds(row, rows), :] + held[j][0, n].astype(F32)
            for h in range(3):
                both = both + final[j][h, n].astype(F32)
            out[n, pl.ds(row, rows), :] = both.astype(BF16)
            return 0

        lax.fori_loop(0, BLOCKS, end, 0)
    back.wait()
    for j in range(3):
        ref = full.at[j] if j < 2 else rest.at[0]
        for c in range(CORES):
            for k in range(SIDE):
                slab = total[j, c, k].astype(F32)
                ref[c, k, :, :, :, pl.ds(0, ROWS)] = slab[:, :, :TERM_ROWS]
                ref[c, k, :, :, :, pl.ds(ROWS, ROWS)] = slab[:, :, TERM_ROWS:]


def return_grads(coeffs, ids, grads, extra, outer, bases, self_grad):
    dma = pltpu.SemaphoreType.DMA
    piece, packed = (TERM_ROWS, WIDTH), (2 * TERM_ROWS, ROWS)
    relations, basis_count = coeffs.shape
    return pl.pallas_call(
        return_kernel,
        out_shape=[
            jax.ShapeDtypeStruct((BLOCKS, ROWS, WIDTH), BF16),
            jax.ShapeDtypeStruct((2, CORES, SIDE, SIDE, SIDE) + piece, F32),
            jax.ShapeDtypeStruct((1, CORES, SIDE, SIDE, SIDE) + piece, F32),
        ],
        in_specs=[SMEM] * 4 + [ANY] * 5,
        out_specs=[VMEM] * 3,
        scratch_shapes=[pltpu.VMEM((CORES, SIDE, SIDE, SIDE, 2, rows, WIDTH), BF16) for *_, rows in PARTS]
        + [pltpu.VMEM((SIDE, SIDE, BLOCKS, rows, WIDTH), BF16) for *_, rows in PARTS]
        + [pltpu.VMEM((2, SIDE, BLOCKS, rows, WIDTH), BF16) for *_, rows in PARTS]
        + [pltpu.VMEM((2, SIDE, BLOCKS // 2, rows, WIDTH), BF16) for *_, rows in PARTS]
        + [pltpu.VMEM((SIDE, BLOCKS, rows, WIDTH), BF16) for *_, rows in PARTS]
        + [pltpu.VMEM((3, BLOCKS, rows, WIDTH), BF16) for *_, rows in PARTS]
        + [
            pltpu.VMEM((BLOCKS, ROWS, WIDTH), F32),
            pltpu.VMEM(outer.shape, F32),
            pltpu.VMEM(bases.shape, BF16),
            pltpu.VMEM((relations * basis_count, 8, ROWS), F32),
            pltpu.VMEM((3, CORES, SIDE, SIDE, SIDE) + piece, F32),
            pltpu.VMEM((3, CORES, SIDE, SIDE, SIDE) + packed, BF16),
            pltpu.VMEM((3, SIDE, SIDE, SIDE) + packed, BF16),
            pltpu.VMEM((3, 3, SIDE, SIDE) + packed, BF16),
            pltpu.VMEM((3, SIDE, SIDE) + packed, BF16),
            pltpu.VMEM((3, 3, SIDE) + packed, BF16),
            pltpu.VMEM((3, SIDE) + packed, BF16),
            pltpu.VMEM((3, 3) + packed, BF16),
            pltpu.VMEM((3, CORES, SIDE, SIDE, SIDE) + packed, BF16),
            dma((3, 7, SIDE)), dma((3, 7, SIDE)), dma((7,)),
            dma((3, 2, SIDE)), dma((3, 2, SIDE)), dma((3, 2, 2, SIDE)), dma((3, 2, 2, SIDE)), dma((3, 3)), dma((3, 3)),
            dma((6,)), dma((6, 3, 3)), dma((6, 3, 3)),
        ],
        compiler_params=pltpu.CompilerParams(collective_id=2, has_side_effects=True, vmem_limit_bytes=60 * MIB),
        name="return_grads",
    )(coeffs, *ids, grads, extra, outer, bases, self_grad)


def piece_specs(steps, start, width):
    size = WIDE // PIECES

    def at(q):
        return lambda i: (jnp.clip(i - start, 0, steps - 1) * PIECES + q, 0, 0)

    return [
        pl.BlockSpec((size, ROWS, width), at(q)) for q in range(PIECES)
    ]


def slot_specs(remote_steps, local_steps):
    return piece_specs(remote_steps, 0, ROWS) + piece_specs(local_steps, remote_steps, ROWS)


def slot_of(pieces, l):
    return pieces[l // (WIDE // PIECES)][l % (WIDE // PIECES)]


def whole(shape):
    return pl.BlockSpec(shape, lambda i: (0,) * len(shape), pipeline_mode=pl.Buffered(1))


def slot_ids(remote, i, l, recv_tgt, recv_rel, recv_count, local_tgt, local_rel):
    if remote:
        peer, c = i * (WIDE // 2) + l // 2, l % 2
        return recv_tgt[c, peer], recv_rel[c, peer], (c < recv_count[0, peer]).astype(F32)
    return local_tgt[0, i * WIDE + l], local_rel[0, i * WIDE + l], 1.0


def degree_kernel(
    recv_tgt, recv_rel, recv_count, local_tgt, local_rel, src, remote_adj, local_adj, cot, scaled, norm,
    total, remote_here, local_here, sem,
):
    lists = (recv_tgt, recv_rel, recv_count, local_tgt, local_rel)
    pairs = ((remote_adj, remote_here), (local_adj, local_here))
    copies = []
    for from_, to in pairs:
        for n in range(from_.shape[0] // WIDE):
            part = pl.ds(n * WIDE, WIDE)
            copies.append(pltpu.make_async_copy(from_.at[part], to.at[part], sem.at[len(copies)]))
            copies[-1].start()
    total[...] = jnp.zeros_like(total)
    done = 0
    for remote_side, (from_, to) in enumerate(pairs):
        for n in range(from_.shape[0] // WIDE):
            copies[done].wait()
            done += 1
            for l in range(WIDE):
                t, r, valid = slot_ids(remote_side == 0, n, l, *lists)
                total[t] += to[n * WIDE + l].astype(F32) * valid
    for t in range(BLOCKS):
        row_norm = lax.rsqrt(1.0 + jnp.sum(total[t], axis=1, keepdims=True))
        scaled[t] = (cot[t].astype(F32) * row_norm).astype(BF16)
        norm[t] = jnp.broadcast_to(row_norm, (ROWS, ROWS))


def degrees(slots, remote_adj, local_adj, cot):
    parts = (remote_adj.shape[0] + local_adj.shape[0]) // WIDE
    return pl.pallas_call(
        degree_kernel,
        out_shape=[
            jax.ShapeDtypeStruct((BLOCKS, ROWS, WIDTH), BF16),
            jax.ShapeDtypeStruct((BLOCKS, ROWS, ROWS), F32),
        ],
        in_specs=[SMEM] * 6 + [ANY] * 2 + [VMEM],
        out_specs=[VMEM] * 2,
        scratch_shapes=[
            pltpu.VMEM((BLOCKS, ROWS, ROWS), F32),
            pltpu.VMEM(remote_adj.shape, BF16),
            pltpu.VMEM(local_adj.shape, BF16),
            pltpu.SemaphoreType.DMA((parts,)),
        ],
        compiler_params=pltpu.CompilerParams(vmem_limit_bytes=58 * MIB),
        name="degrees",
    )(*slots, remote_adj, local_adj, cot)


def forward_kernel(
    remote_steps, recv_tgt, recv_rel, recv_count, local_tgt, local_rel, src, *refs,
):
    remote_adj, local_adj, incoming = (refs[n * PIECES : (n + 1) * PIECES] for n in range(3))
    feats, weights, scaled, norm, self_out, out, outer, mixed, held = refs[3 * PIECES :]
    i = pl.program_id(0)
    lists = (recv_tgt, recv_rel, recv_count, local_tgt, local_rel)

    @pl.when(i == 0)
    def _():
        mixed[...] = jnp.zeros_like(mixed)
        outer[...] = jnp.zeros_like(outer)

    def visit(remote, step, adj, rows_of):
        for l in range(WIDE):
            t, r, valid = slot_ids(remote, step, l, *lists)
            held[l] = (jnp.dot(slot_of(adj, l), rows_of(l), preferred_element_type=F32) * valid).astype(BF16)
        for l in range(WIDE):
            t, r, valid = slot_ids(remote, step, l, *lists)
            mixed[t] += jnp.dot(held[l], weights[r], preferred_element_type=F32)
            outer[r] += lax.dot_general(held[l], scaled[t], (((0,), (0,)), ((), ())), preferred_element_type=F32)

    @pl.when(i < remote_steps)
    def _():
        visit(True, i, remote_adj, lambda l: slot_of(incoming, l))

    @pl.when(i >= remote_steps)
    def _():
        step = i - remote_steps
        visit(False, step, local_adj, lambda l: feats[src[0, step * WIDE + l]])

    @pl.when(i == pl.num_programs(0) - 1)
    def _():
        for t in range(BLOCKS):
            for half in range(2):
                cols = pl.ds(half * ROWS, ROWS)
                out[t, :, cols] = (norm[t] * mixed[t, :, cols] + self_out[t, :, cols]).astype(BF16)


def forward_slots(slots, remote_adj, local_adj, incoming, feats, weights, scaled, norm, self_out):
    remote_steps, local_steps = remote_adj.shape[0] // WIDE, local_adj.shape[0] // WIDE
    relations = weights.shape[0]
    return pl.pallas_call(
        functools.partial(forward_kernel, remote_steps),
        grid=(remote_steps + local_steps,),
        out_shape=[
            jax.ShapeDtypeStruct((BLOCKS, ROWS, WIDTH), BF16),
            jax.ShapeDtypeStruct((relations, WIDTH, WIDTH), F32),
        ],
        in_specs=[SMEM] * 6
        + slot_specs(remote_steps, local_steps)
        + piece_specs(remote_steps, 0, WIDTH)
        + [whole(a.shape) for a in (feats, weights, scaled, norm, self_out)],
        out_specs=[whole((BLOCKS, ROWS, WIDTH)), whole((relations, WIDTH, WIDTH))],
        scratch_shapes=[pltpu.VMEM((BLOCKS, ROWS, WIDTH), F32), pltpu.VMEM((WIDE, ROWS, WIDTH), BF16)],
        compiler_params=pltpu.CompilerParams(vmem_limit_bytes=58 * MIB),
        name="forward_slots",
    )(
        *slots, *[remote_adj] * PIECES, *[local_adj] * PIECES, *[incoming] * PIECES, feats, weights, scaled, norm,
        self_out,
    )


def local(
    node_feats, send_block, recv_block, recv_rel, recv_count, recv_adj, local_src, local_tgt, local_rel, local_adj,
    bases, coeffs, self_weight, cotangent,
):
    peers = lax.axis_size(("src", "tgt"))
    slot_cap = send_block.shape[2]
    remote_slots = peers * slot_cap
    relations, basis_count = coeffs.shape
    feats = node_feats.reshape(BLOCKS, ROWS, WIDTH)
    cot = cotangent.reshape(BLOCKS, ROWS, WIDTH)
    remote_adj = recv_adj.reshape(remote_slots, ROWS, ROWS)
    own_adj = local_adj[0]
    slots = (recv_block[0].T, recv_rel[0].T, recv_count, local_tgt, local_rel, local_src)
    wide_coeffs = coeffs.astype(F32)
    scaled, norm = degrees(slots, remote_adj, own_adj, cot)
    incoming, *ids, weights, extra, grads, self_out, self_grad = spread_features(
        wide_coeffs, slots, feats, send_block[0].T, bases, scaled, cot, self_weight, remote_adj, own_adj
    )
    incoming = incoming.reshape(remote_slots, ROWS, WIDTH)
    features_out, outer = forward_slots(slots, remote_adj, own_adj, incoming, feats, weights, scaled, norm, self_out)
    grad_features, grad_bases, rest = return_grads(
        wide_coeffs,
        ids,
        grads.reshape(SIDE, CORES, SIDE, SIDE, slot_cap, ROWS, WIDTH),
        extra,
        outer,
        bases,
        self_grad.reshape(2, SIDE, SIDE, TERM_ROWS, WIDTH),
    )
    scale = 1.0 / math.sqrt(node_feats.shape[0] * peers)
    rest = rest.reshape(-1, WIDTH)
    coef = rest[WIDTH : WIDTH + relations * basis_count, :ROWS]
    return (
        features_out.reshape(node_feats.shape),
        grad_features.reshape(node_feats.shape),
        grad_bases.reshape(bases.shape) * scale,
        jnp.sum(coef, axis=1).reshape(relations, basis_count) * scale,
        rest[:WIDTH] * scale,
    )


def solution(mesh):
    both = ("src", "tgt")
    in_specs = (
        P(both, None),
        P(both, None, None),
        P(both, None, None),
        P(both, None, None),
        P(both, None),
        P(both, None, None, None, None),
        P(both, None),
        P(both, None),
        P(both, None),
        P(both, None, None, None),
        P(),
        P(),
        P(),
        P(both, None),
    )
    out_specs = (P(both, None), P(both, None), P(), P(), P())
    return jax.shard_map(local, mesh=mesh, in_specs=in_specs, out_specs=out_specs, check_vma=False)
```

time: 354 us -> 300 us (0.85)
  Pallas kernels: 327 us -> 290 us
  local copies, waits for them, and re-layouts: 21.5 us -> 2.33 us
    pallas_call x1, Pallas kernels: 147 us -> 130 us  [return_grads(): pl.pallas_call(return_kernel, out_shape=[jax.ShapeDtypeStruct((BLOCKS, RO...]
    pallas_call x3 -> x2, Pallas kernels: 137 us -> 122 us  [the longest x1 116 us: spread_features(): pl.pallas_call(spread_kernel, out_shape=[jax.ShapeDtypeStruct((SIDE, CORE...]
    unnamed x51 -> x5, local copies, waits for them, and re-layouts: 16.3 us -> 2.25 us
    pallas_call x1, Pallas kernels: 42.6 us -> 36.9 us  [forward_slots(): pl.pallas_call(functools.partial(forward_kernel, remote_steps), grid=(rem...]
    mul x0 -> x3, other arithmetic: none -> 5.03 us  [the longest x1 3.35 us: local(): grad_bases.reshape(bases.shape) * scale]
    slice x2 -> x0, local copies, waits for them, and re-layouts: 4.71 us -> none  [the longest x1 3.04 us: local(): totals[:basis_rows].reshape(basis_count, WIDTH, WIDTH)]
where the time goes in v3:
time: 300 us; the launch traced here: 299 us
  Pallas kernels  290 us (97%)
  other arithmetic  6.65 us (2%)
    pallas_call x1, Pallas kernels, return_grads(): pl.pallas_call(return_kernel, out_shape=[jax.ShapeDtypeStruct((BLOCKS, RO...  130 us
    pallas_call x1, Pallas kernels, spread_features(): pl.pallas_call(spread_kernel, out_shape=[jax.ShapeDtypeStruct((SIDE, CORE...  116 us
    pallas_call x1, Pallas kernels, forward_slots(): pl.pallas_call(functools.partial(forward_kernel, remote_steps), grid=(rem...  36.9 us
    pallas_call x1, Pallas kernels, degrees(): pl.pallas_call(degree_kernel, out_shape=[jax.ShapeDtypeStruct((BLOCKS, RO...  6.54 us

profile of v3, /device:TPU:1, one launch (start us, length us, event | category | flops | bytes accessed | tf_op | source)
XLA Modules:
  0.0 299.2 jit_solution(3511268038301160164)
XLA Ops:
  0.6 0.8 copy.20
  1.4 0.6 convert_element_type.3.coeffs
  2.0 6.5 %degrees.1 = (bf16[8,128,256]{2,1,0:T(8,128)(2,1)}, f32[8,128,128]{2,1,0:T(8,128)}) custom-call(s32[2,128]{1,0:T(2,128)} %bitcast.46, s32[2,128]{1,0:T(2,128)} %bitcast.49, s32[1,128]{1,0:T(1,128)} %recv_count.5, s32[1,64]{1,0:T(1,128)} %local_tgt.5, s32[1,64]{1,0:T(1,128)} %local_rel.5, s32[1,64]{1,0:T(1,128)} %src.5, bf16[256,128,128]{2,1,0:T(8,128)(2,1)} %bitcast.20, ...), custom_call_target="tpu_custom_call" | custom-call | tf_op jit(solution)/shard_map/degrees/pallas_call | solution.py:724
  8.6 115.6 %spread_features.1 = (bf16[4,2,4,4,2,128,256]{6,5,4,3,2,1,0:T(8,128)(2,1)}, s32[4,4,2,128]{3,2,1,0:T(2,128)}, s32[4,4,2,128]{3,2,1,0:T(2,128)}, s32[4,4,2,128]{3...) custom-call(f32[30,8]{1,0:T(8,128)} %convert_element_type.3.coeffs, ...), custom_call_target="tpu_custom_call" | custom-call | tf_op jit(solution)/shard_map/spread_features/pallas_call | solution.py:333
  124.2 36.9 %forward_slots.1 = (bf16[8,128,256]{2,1,0:T(8,128)(2,1)}, f32[30,256,256]{2,1,0:T(8,128)}) custom-call(s32[2,128]{1,0:T(2,128)} %bitcast.48, s32[2,128]{1,0:T(2,128)} %bitcast.51, s32[1,128]{1,0:T(1,128)} %recv_count.5, s32[1,64]{1,0:T(1,128)} %local_tgt.5, s32[1,64]{1,0:T(1,128)} %local_rel.5, s32[1,64]{1,0:T(1,128)} %src.5, ...), custom_call_target="tpu_custom_call" | custom-call | tf_op jit(solution)/shard_map/forward_slots/pallas_call | solution.py:785
  161.1 130.5 %return_grads.1 = (bf16[8,128,256]{2,1,0:T(8,128)(2,1)}, f32[2,2,4,4,4,8,256]{6,5,4,3,2,1,0:T(8,128)}, f32[1,2,4,4,4,8,256]{6,5,4,3,2,1,0:T(8,128)}) custom-call(f32[30,8]{1,0:T(8,128)} %convert_element_type.3.coeffs, s32[4,4,2,128]{3,2,1,0:T(2,128)} %get-tuple-element.27.i0, s32[4,4,2,128]{3,2,1,0:T(2,128)} %get-tuple-element.28.i1, ...), custom_call_target="tpu_custom_call" | custom-call | tf_op jit(solution)/shard_map/return_grads/pallas_call | solution.py:627
  291.6 1.0 slice_reduce_fusion
  292.6 1.7 slice_multiply_fusion
  294.3 0.1 mul.29
  294.4 0.7 copy.21
  295.0 0.0 copy-start
  295.1 3.4 %broadcast_multiply_fusion = f32[2,2,4,4,4,8,256]{6,5,4,3,2,1,0:T(8,128)} fusion(f32[2,2,4,4,4,8,256]{6,5,4,3,2,1,0:T(8,128)} %get-tuple-element.35), kind=kLoop, calls=%fused_computation | loop fusion | flops 524288 | bytes 4194304 | tf_op jit(solution)/shard_map/mul | solution.py:841
  298.4 0.0 copy-done
  298.4 0.8 copy.23
  (1 shorter events, 0.0 us)
Async XLA Ops:
  295.0 3.4 %copy-start = (bf16[8,128,256]{2,1,0:T(8,128)(2,1)S(1)}, bf16[8,128,256]{2,1,0:T(8,128)(2,1)}, u32[]{:S(2)}) copy-start(bf16[8,128,256]{2,1,0:T(8,128)(2,1)} %get-tuple-element.34) | copy-start | bytes 1572868

commit v4 on v3

--- a/solution.py
+++ b/solution.py
@@ -19,7 +19,7 @@
 WIDTH = 256
 STEP = 8
 WIDE = 32
-PIECES = 4
+PIECES = 1
 CHUNKS = 8
 TERM_ROWS = 8
 PARTS = (("x", "y", "z", 0, 48), ("y", "z", "x", 48, 48), ("z", "x", "y", 96, 32))
@@ -541,36 +541,41 @@
                 wire[j, c, k] = jnp.concatenate([slab[..., :ROWS], slab[..., ROWS:]], axis=2).astype(BF16)
     halves = remote(wire.at[:, partner["c"]], b0, pair_sem.at[0], pair_sem.at[1], partner)
     halves.start()
-    give(3)
     done(own[3:])
-    done(sent[2])
-    each_band(far_bands)
     halves.wait()
     b0[...] = add(wire[:, core], b0[...]).astype(BF16)
     stage = weigh(0, 2, lambda j, k: b0.at[j, k], lambda j, h: b1.at[j, h])
+    give(3)
+    done(sent[2])
+    done(stage)
+    for j, part in enumerate(PARTS):
+        h1[j] = add(b0[j, me[part[2]]], b1[j, 0], b1[j, 1], b1[j, 2]).astype(BF16)
+    stage = weigh(1, 1, lambda j, k: h1.at[j, k], lambda j, h: b2.at[j, h])
+    each_band(far_bands)
+    done(stage)
+    for j, part in enumerate(PARTS):
+        h2[j] = add(h1[j, me[part[1]]], b2[j, 0], b2[j, 1], b2[j, 2]).astype(BF16)
+    stage = weigh(2, 0, lambda j, k: h2.at[j, k], lambda j, h: b3.at[j, h])
+    done(stage)
+    for j, part in enumerate(PARTS):
+        piece(j, 3)[...] = add(h2[j, me[part[0]]], b3[j, 0], b3[j, 1], b3[j, 2]).astype(BF16)
+    stage = weigh(3, 0, lambda j, k: piece(j, 3), lambda j, h: piece(j, 3))
     give(0)
     done(sent[1])
     each_band(near_bands(0, 0))
     done(stage)
-    for j, part in enumerate(PARTS):
-        h1[j] = add(b0[j, me[part[2]]], b1[j, 0], b1[j, 1], b1[j, 2]).astype(BF16)
-    stage = weigh(1, 1, lambda j, k: h1.at[j, k], lambda j, h: b2.at[j, h])
+    stage = weigh(4, 1, lambda j, k: piece(j, 2), lambda j, h: piece(j, 2))
     done(sent[3])
     each_band(near_bands(1, 0))
     done(stage)
-    for j, part in enumerate(PARTS):
-        h2[j] = add(h1[j, me[part[1]]], b2[j, 0], b2[j, 1], b2[j, 2]).astype(BF16)
-    stage = weigh(2, 0, lambda j, k: h2.at[j, k], lambda j, h: b3.at[j, h])
+    stage = weigh(5, 2, lambda j, k: piece(j, 1), lambda j, h: piece(j, 1))
     each_band(near_bands(0, 1))
     each_band(near_bands(1, 1))
-    done(stage)
-    for j, part in enumerate(PARTS):
-        piece(j, 3)[...] = add(h2[j, me[part[0]]], b3[j, 0], b3[j, 1], b3[j, 2]).astype(BF16)
-    stage = weigh(3, 0, lambda j, k: piece(j, 3), lambda j, h: piece(j, 3))
     done(sent[0])
     each_band(lambda j, k: fold(j, 0, k, 0, BLOCKS))
     done(stage)
-    stage = weigh(4, 1, lambda j, k: piece(j, 2), lambda j, h: piece(j, 2))
+    back = remote(total.at[:, core], total.at[:, core], pair_sem.at[2], pair_sem.at[3], partner)
+    back.start()
     for j in range(3):
         for way in range(2):
             for late in range(2):
@@ -594,12 +599,7 @@
                 )
                 copy.start()
                 second.append(copy)
-    done(stage)
-    stage = weigh(5, 2, lambda j, k: piece(j, 1), lambda j, h: piece(j, 1))
     done(second)
-    done(stage)
-    back = remote(total.at[:, core], total.at[:, core], pair_sem.at[2], pair_sem.at[3], partner)
-    back.start()
     for j, (a1, a2, last, row, rows) in enumerate(PARTS):
 
         def end(n, _, j=j, row=row, rows=rows):

time: 300 us -> 295 us (0.983)
  Pallas kernels: 290 us -> 284 us
    pallas_call x1, Pallas kernels: 130 us -> 126 us  [return_grads(): pl.pallas_call(return_kernel, out_shape=[jax.ShapeDtypeStruct((BLOCKS, RO...]
where the time goes in v4:
time: 295 us; the launch traced here: 293 us
  Pallas kernels  284 us (96%)
  other arithmetic  6.65 us (2%)
    pallas_call x1, Pallas kernels, return_grads(): pl.pallas_call(return_kernel, out_shape=[jax.ShapeDtypeStruct((BLOCKS, RO...  126 us
    pallas_call x1, Pallas kernels, spread_features(): pl.pallas_call(spread_kernel, out_shape=[jax.ShapeDtypeStruct((SIDE, CORE...  116 us
    pallas_call x1, Pallas kernels, forward_slots(): pl.pallas_call(functools.partial(forward_kernel, remote_steps), grid=(rem...  35.8 us
    pallas_call x1, Pallas kernels, degrees(): pl.pallas_call(degree_kernel, out_shape=[jax.ShapeDtypeStruct((BLOCKS, RO...  6.55 us

profile of v4, /device:TPU:1, one launch (start us, length us, event | category | flops | bytes accessed | tf_op | source)
XLA Modules:
  0.0 293.4 jit_solution(8487444032369784942)
XLA Ops:
  0.6 0.8 copy.20
  1.4 0.6 convert_element_type.3.coeffs
  2.0 6.5 %degrees.1 = (bf16[8,128,256]{2,1,0:T(8,128)(2,1)}, f32[8,128,128]{2,1,0:T(8,128)}) custom-call(s32[2,128]{1,0:T(2,128)} %bitcast.37, s32[2,128]{1,0:T(2,128)} %bitcast.40, s32[1,128]{1,0:T(1,128)} %recv_count.5, s32[1,64]{1,0:T(1,128)} %local_tgt.5, s32[1,64]{1,0:T(1,128)} %local_rel.5, s32[1,64]{1,0:T(1,128)} %src.5, bf16[256,128,128]{2,1,0:T(8,128)(2,1)} %bitcast.20, ...), custom_call_target="tpu_custom_call" | custom-call | tf_op jit(solution)/shard_map/degrees/pallas_call | solution.py:724
  8.6 115.6 %spread_features.1 = (bf16[4,2,4,4,2,128,256]{6,5,4,3,2,1,0:T(8,128)(2,1)}, s32[4,4,2,128]{3,2,1,0:T(2,128)}, s32[4,4,2,128]{3,2,1,0:T(2,128)}, s32[4,4,2,128]{3...) custom-call(f32[30,8]{1,0:T(8,128)} %convert_element_type.3.coeffs, ...), custom_call_target="tpu_custom_call" | custom-call | tf_op jit(solution)/shard_map/spread_features/pallas_call | solution.py:333
  124.2 35.8 %forward_slots.1 = (bf16[8,128,256]{2,1,0:T(8,128)(2,1)}, f32[30,256,256]{2,1,0:T(8,128)}) custom-call(s32[2,128]{1,0:T(2,128)} %bitcast.39, s32[2,128]{1,0:T(2,128)} %bitcast.42, s32[1,128]{1,0:T(1,128)} %recv_count.5, s32[1,64]{1,0:T(1,128)} %local_tgt.5, s32[1,64]{1,0:T(1,128)} %local_rel.5, s32[1,64]{1,0:T(1,128)} %src.5, ...), custom_call_target="tpu_custom_call" | custom-call | tf_op jit(solution)/shard_map/forward_slots/pallas_call | solution.py:785
  160.0 125.8 %return_grads.1 = (bf16[8,128,256]{2,1,0:T(8,128)(2,1)}, f32[2,2,4,4,4,8,256]{6,5,4,3,2,1,0:T(8,128)}, f32[1,2,4,4,4,8,256]{6,5,4,3,2,1,0:T(8,128)}) custom-call(f32[30,8]{1,0:T(8,128)} %convert_element_type.3.coeffs, s32[4,4,2,128]{3,2,1,0:T(2,128)} %get-tuple-element.27.i0, s32[4,4,2,128]{3,2,1,0:T(2,128)} %get-tuple-element.28.i1, ...), custom_call_target="tpu_custom_call" | custom-call | tf_op jit(solution)/shard_map/return_grads/pallas_call | solution.py:627
  285.8 1.0 slice_reduce_fusion
  286.9 1.7 slice_multiply_fusion
  288.5 0.1 mul.29
  288.6 0.7 copy.21
  289.3 0.0 copy-start
  289.3 3.4 %broadcast_multiply_fusion = f32[2,2,4,4,4,8,256]{6,5,4,3,2,1,0:T(8,128)} fusion(f32[2,2,4,4,4,8,256]{6,5,4,3,2,1,0:T(8,128)} %get-tuple-element.35), kind=kLoop, calls=%fused_computation | loop fusion | flops 524288 | bytes 4194304 | tf_op jit(solution)/shard_map/mul | solution.py:841
  292.7 0.0 copy-done
  292.7 0.8 copy.23
  (1 shorter events, 0.0 us)
Async XLA Ops:
  289.3 3.4 %copy-start = (bf16[8,128,256]{2,1,0:T(8,128)(2,1)S(1)}, bf16[8,128,256]{2,1,0:T(8,128)(2,1)}, u32[]{:S(2)}) copy-start(bf16[8,128,256]{2,1,0:T(8,128)(2,1)} %get-tuple-element.34) | copy-start | bytes 1572868
